TPU v7x, 512 devices: a whole 4x4x16 slice. The times are simulated.
512 devices in a mesh: inst: 16 (over y, x), label: 32 (over z, core).
Axes of the slice: x: 4, y: 4, z: 16, core: 2. Of those that a mesh axis runs over, the one named last changes fastest.
Arguments:
- features: bfloat16 [65536, 768], P(('inst', 'label')), may hold values from -6 to 6
- weights: bfloat16 [32768, 768], P('label'), may hold values from -0.21875 to 0.21875
- block_ids: int32 [65536, 16], P(('inst', 'label')), may hold values from 0 to 255, all different within a row; in each aligned block of 128 rows (0 to 127, 128 to 255, ...) at most 16 rows name the same one
- label_codes: int32 [65536, 16], P(('inst', 'label')), may hold values from 0 to 255
- counts: int32 [65536], P(('inst', 'label')), may hold values from 12 to 16
Outputs:
- grad_x: bfloat16 [65536, 768], P(('inst', 'label'))
- grad_w: float32 [32768, 768], P(('label', 'inst'))
- grad_logits: bfloat16 [65536, 16, 128], P(('inst', 'label'))
Inputs may be any that keep to these rules, and one draw needn't show every extreme that they name: `block_ids`: each row names 16 different blocks; in the rows of one device no block is named by more than 16 rows, and some block reaches 16. `label_codes`: A code below 128 is the offset of the positive cluster in the slot's block; a code of 128 or more marks a hard negative block. Slots at index counts[n] or beyond are padding.
All inputs are finite; a program needn't handle non-finite values.
Results may differ from a plain program's by a relative error of at most 0.014.
Values may be sent and summed in bfloat16 or wider, within the bound.
No kernel may reach another device: no remote copies, remote signals or barrier semaphores. Data moves between devices by JAX's collectives and lax.ppermute only.
A program may use at most 64 MiB of HBM per device.

v0:
```python
import jax
import jax.numpy as jnp
from jax import lax
from jax.sharding import PartitionSpec as P

BS = 128
MOST = 16


def bucket_slots(flat_ids, block_total):
    one_hot = (flat_ids[:, None] == jnp.arange(block_total, dtype=jnp.int32)[None, :]).astype(
        jnp.int32
    )
    rank_within = jnp.sum((jnp.cumsum(one_hot, axis=0) - one_hot) * one_hot, axis=1)
    return flat_ids * MOST + rank_within


def shards(features, weights, block_ids, label_codes, counts):
    row_count = features.shape[0]
    slot_count = block_ids.shape[1]
    feature_dim = features.shape[1]
    label_size = lax.axis_size("label")
    shard_blocks = weights.shape[0] // BS
    block_total = shard_blocks * label_size
    pair_count = row_count * slot_count
    slot_numbers = jnp.arange(slot_count, dtype=jnp.int32)[None, :]
    pair_codes = jnp.where(slot_numbers < counts[:, None], label_codes, -1)
    slot_index = bucket_slots(block_ids.reshape(-1), block_total)
    block_weights = weights.reshape(shard_blocks, BS, feature_dim)
    pair_numbers = jnp.arange(pair_count, dtype=jnp.int32)
    bucket_table = (
        jnp.full((block_total * MOST,), pair_count, jnp.int32).at[slot_index].set(pair_numbers)
    )
    padded_rows = jnp.concatenate([features, jnp.zeros((1, feature_dim), features.dtype)], 0)
    pair_rows = jnp.concatenate([pair_numbers // slot_count, jnp.full((1,), row_count, jnp.int32)])
    padded_codes = jnp.concatenate([pair_codes.reshape(-1), jnp.full((1,), -1, jnp.int32)])
    sent_rows = padded_rows[pair_rows[bucket_table]].reshape(
        label_size, shard_blocks, MOST, feature_dim
    )
    sent_codes = (
        padded_codes[bucket_table].astype(jnp.bfloat16).reshape(label_size, shard_blocks, MOST)
    )
    got_rows, got_codes = (
        lax.all_to_all(sent_rows, "label", split_axis=0, concat_axis=0, tiled=True),
        lax.all_to_all(sent_codes, "label", split_axis=0, concat_axis=0, tiled=True),
    )
    got_codes = got_codes.astype(jnp.int32)
    offsets = jnp.arange(BS, dtype=jnp.int32)
    logits = jnp.einsum(
        "sbmd,bcd->sbmc", got_rows, block_weights, preferred_element_type=jnp.float32
    )
    target = (got_codes[..., None] == offsets).astype(jnp.float32)
    alive_mask = (got_codes >= 0).astype(jnp.float32)[..., None]
    logit_grad = (alive_mask * (jax.nn.sigmoid(logits) - target)).astype(jnp.bfloat16)
    slot_grads = jnp.einsum(
        "sbmc,bcd->sbmd", logit_grad, block_weights, preferred_element_type=jnp.float32
    ).astype(jnp.bfloat16)
    local_weight = jnp.einsum(
        "sbmc,sbmd->bcd", logit_grad, got_rows, preferred_element_type=jnp.float32
    ).reshape(shard_blocks * BS, feature_dim)
    back_logits, back_slots = (
        lax.all_to_all(logit_grad, "label", split_axis=0, concat_axis=0, tiled=True),
        lax.all_to_all(slot_grads, "label", split_axis=0, concat_axis=0, tiled=True),
    )
    flat_logits = back_logits.reshape(block_total * MOST, BS)
    flat_slots = back_slots.reshape(block_total * MOST, feature_dim)
    grad_logits = flat_logits[slot_index].reshape(row_count, slot_count, BS)
    picked = flat_slots[slot_index].reshape(row_count, slot_count, feature_dim)
    grad_x = jnp.sum(picked, axis=1, dtype=jnp.float32).astype(jnp.bfloat16)
    grad_w = lax.psum_scatter(
        local_weight.astype(jnp.bfloat16), "inst", scatter_dimension=0, tiled=True
    ).astype(jnp.float32)
    return (grad_x, grad_w, grad_logits)


def solution(mesh):
    in_specs = (
        P(("inst", "label"), None),
        P("label", None),
        P(("inst", "label"), None),
        P(("inst", "label"), None),
        P(("inst", "label")),
    )
    out_specs = (
        P(("inst", "label"), None),
        P(("label", "inst"), None),
        P(("inst", "label"), None, None),
    )
    return jax.shard_map(shards, mesh=mesh, in_specs=in_specs, out_specs=out_specs, check_vma=False)
```

profile of v0, /device:TPU:34, one launch (start us, length us, event | category | flops | bytes accessed | tf_op | source)
XLA Modules:
  0.0 771.4 jit_solution(2868056716338270478)
XLA Ops:
  7.2 0.0 copy-start
  7.2 0.8 broadcast_multiply_fusion
  8.0 0.8 copy.50
  8.8 0.1 eq.42
  8.9 0.1 eq.38
  9.0 0.1 copy.49
  9.1 0.1 mul.29
  9.2 0.7 fusion.20
  9.9 0.1 copy.48
  10.0 0.1 reshape.94
  10.0 0.1 copy.52
  10.1 0.3 fusion.8
  10.5 0.0 copy-start.1
  10.5 1.3 copy-done.1
  11.9 1.8 broadcast_add_fusion
  13.7 1.2 copy.53
  14.9 0.9 fusion.5
  15.9 8.1 %scatter_custom_fusion = s32[4096]{0:T(1024)S(1)} fusion(s32[2048]{0:T(1024)S(1)} %bitcast.51, s32[2048]{0:T(1024)S(1)} %iota.21, s32[]{:T(128)} %constant.16.clone.1), kind=kCustom, calls=%fused_computation.41 | custom fusion | bytes 16388 | tf_op jit(solution)/shard_map/scatter | solution.py:32
  24.0 23.0 %gather_fusion = s32[4096]{0:T(1024)S(1)} fusion(s32[2049]{0:T(1024)S(1)} %pad_add_fusion, s32[4096]{0:T(1024)S(1)} %fusion.15), kind=kCustom, calls=%fused_computation | custom fusion | bytes 49152 | tf_op jit(solution)/shard_map/gather | solution.py:41
  47.1 0.7 convert_element_type.46
  47.8 15.4 %all-to-all-start = ((bf16[32,8,16]{2,1,0:T(8,128)(2,1)}), bf16[32,8,16]{2,1,0:T(8,128)(2,1)S(1)}, u32[]{:S(2)}, u32[]{:S(2)}) async-start(bf16[32,8,16]{2,1,0:T(8,128)(2,1)} %convert_element_type.46), calls=%async_computation | async-start | bytes 131072 | tf_op jit(solution)/shard_map/all_to_all | solution.py:45
  63.2 0.0 copy-start.3
  63.2 23.0 %gather_fusion.1 = s32[4096]{0:T(1024)S(1)} fusion(s32[2049]{0:T(1024)S(1)} %pad_add_fusion.1, s32[4096]{0:T(1024)S(1)} %fusion.15), kind=kCustom, calls=%fused_computation.1 | custom fusion | bytes 49152 | tf_op jit(solution)/shard_map/gather | solution.py:37
  86.3 0.0 copy-done.3
  86.3 17.8 %gather_fusion.2 = bf16[4096,768]{1,0:T(8,128)(2,1)} fusion(bf16[129,768]{1,0:T(8,128)(2,1)S(1)} %concatenate.10, s32[4096]{0:T(1024)S(1)} %broadcast_clamp_fusion), kind=kCustom, calls=%fused_computation.2 | custom fusion | bytes 12599296 | tf_op jit(solution)/shard_map/gather | solution.py:37
  104.1 0.0 all-to-all-done
  104.1 12.2 %all-to-all-start.1 = ((bf16[32,8,16,768]{3,2,1,0:T(8,128)(2,1)}), bf16[32,8,16,768]{3,2,1,0:T(8,128)(2,1)}, u32[]{:S(2)}, u32[]{:S(2)}) async-start(bf16[32,8,16,768]{3,2,1,0:T(8,128)(2,1)} %bitcast.45), calls=%async_computation.1 | async-start | bytes 12582912 | tf_op jit(solution)/shard_map/all_to_all | solution.py:44
  116.3 0.1 copy.54
  116.5 0.1 copy.57
  116.6 0.1 copy.55
  116.7 279.7 %all-to-all-done.1 = bf16[32,8,16,768]{3,2,1,0:T(8,128)(2,1)} async-done(((bf16[32,8,16,768]{3,2,1,0:T(8,128)(2,1)}), bf16[32,8,16,768]{3,2,1,0:T(8,128)(2,1)}, u32[]{:S(2)}, u32[]{:S(2)}) %all-to-all-start.1) | async-done | bytes 6291488 | tf_op jit(solution)/shard_map/all_to_all | solution.py:44
  396.4 0.0 copy-done
  396.4 4.0 fusion.7
  400.4 0.0 copy-start.2
  400.4 0.9 copy-done.2
  401.3 1.3 copy.60
  402.6 3.7 all-to-all-start.3
  406.4 3.0 convert_bitcast_fusion
  409.4 3.5 copy.58
  412.9 47.3 %all-to-all-done.3 = bf16[32,8,16,128]{3,2,1,0:T(8,128)(2,1)S(1)} async-done(((bf16[32,8,16,128]{3,2,1,0:T(8,128)(2,1)}), bf16[32,8,16,128]{3,2,1,0:T(8,128)(2,1)S(1)}, u32[]{:S(2)}, u32[]{:S(2)}) %all-to-all-start.3) | async-done | bytes 1048608 | tf_op jit(solution)/shard_map/all_to_all | solution.py:62
  460.2 6.6 all-to-all-start.2
  466.8 0.2 reduce-scatter.2.cloned.1.call-start
  467.0 5.4 bitcast_convert_fusion
  472.4 0.0 reduce-scatter.2.cloned.1.call-update
  472.5 89.8 %reduce-scatter.2.cloned.1.call-done = bf16[64,768]{1,0:T(8,128)(2,1)} async-done(((bf16[1024,768]{1,0:T(8,128)(2,1)}), bf16[64,768]{1,0:T(8,128)(2,1)}) %reduce-scatter.2.cloned.1.call-update) | async-done | bytes 98320 | tf_op jit(solution)/shard_map/reduce_scatter | solution.py:70
  562.3 1.6 convert_element_type.55
  563.9 8.0 %gather_fusion.4 = bf16[2048,128]{1,0:T(8,128)(2,1)} fusion(bf16[4096,128]{1,0:T(8,128)(2,1)S(1)} %bitcast.44, s32[2048]{0:T(1024)S(1)} %broadcast_clamp_fusion.1), kind=kCustom, calls=%fused_computation.4 | custom fusion | bytes 1056768 | tf_op jit(solution)/shard_map/gather | solution.py:67
  571.9 175.1 %all-to-all-done.2 = bf16[32,8,16,768]{3,2,1,0:T(8,128)(2,1)} async-done(((bf16[32,8,16,768]{3,2,1,0:T(8,128)(2,1)}), bf16[32,8,16,768]{3,2,1,0:T(8,128)(2,1)}, u32[]{:S(2)}, u32[]{:S(2)}) %all-to-all-start.2) | async-done | bytes 6291488 | tf_op jit(solution)/shard_map/all_to_all | solution.py:63
  747.0 13.7 %gather_fusion.3 = bf16[2048,768]{1,0:T(8,128)(2,1)} fusion(bf16[4096,768]{1,0:T(8,128)(2,1)} %bitcast.13, s32[2048]{0:T(1024)S(1)} %broadcast_clamp_fusion.1), kind=kCustom, calls=%fused_computation.3 | custom fusion | bytes 6299648 | tf_op jit(solution)/shard_map/gather | solution.py:68
  760.7 3.8 bitcast_reduce_fusion
  (16 shorter events, 0.2 us)
Async XLA Ops:
  7.2 389.2 %copy-start = (bf16[1024,768]{1,0:T(8,128)(2,1)S(1)}, bf16[1024,768]{1,0:T(8,128)(2,1)}, u32[]{:S(2)}) copy-start(bf16[1024,768]{1,0:T(8,128)(2,1)} %param.6) | copy-start | bytes 4718596
  10.5 1.4 copy-start.1
  47.8 56.3 %all-to-all-start = ((bf16[32,8,16]{2,1,0:T(8,128)(2,1)}), bf16[32,8,16]{2,1,0:T(8,128)(2,1)S(1)}, u32[]{:S(2)}, u32[]{:S(2)}) async-start(bf16[32,8,16]{2,1,0:T(8,128)(2,1)} %convert_element_type.46), calls=%async_computation | async-start | bytes 131072 | tf_op jit(solution)/shard_map/all_to_all | solution.py:45
  63.2 23.1 %copy-start.3 = (bf16[128,768]{1,0:T(8,128)(2,1)S(1)}, bf16[128,768]{1,0:T(8,128)(2,1)}, u32[]{:S(2)}) copy-start(bf16[128,768]{1,0:T(8,128)(2,1)} %param.5) | copy-start | bytes 589828
  104.1 292.3 %all-to-all-start.1 = ((bf16[32,8,16,768]{3,2,1,0:T(8,128)(2,1)}), bf16[32,8,16,768]{3,2,1,0:T(8,128)(2,1)}, u32[]{:S(2)}, u32[]{:S(2)}) async-start(bf16[32,8,16,768]{3,2,1,0:T(8,128)(2,1)} %bitcast.45), calls=%async_computation.1 | async-start | bytes 12582912 | tf_op jit(solution)/shard_map/all_to_all | solution.py:44
  400.4 1.0 copy-start.2
  402.6 57.6 %all-to-all-start.3 = ((bf16[32,8,16,128]{3,2,1,0:T(8,128)(2,1)}), bf16[32,8,16,128]{3,2,1,0:T(8,128)(2,1)S(1)}, u32[]{:S(2)}, u32[]{:S(2)}) async-start(bf16[32,8,16,128]{3,2,1,0:T(8,128)(2,1)} %copy.60), calls=%async_computation.4 | async-start | bytes 2097152 | tf_op jit(solution)/shard_map/all_to_all | solution.py:62
  460.2 286.8 %all-to-all-start.2 = ((bf16[32,8,16,768]{3,2,1,0:T(8,128)(2,1)}), bf16[32,8,16,768]{3,2,1,0:T(8,128)(2,1)}, u32[]{:S(2)}, u32[]{:S(2)}) async-start(bf16[32,8,16,768]{3,2,1,0:T(8,128)(2,1)} %copy.58), calls=%async_computation.2 | async-start | bytes 12582912 | tf_op jit(solution)/shard_map/all_to_all | solution.py:63
  466.8 95.5 %reduce-scatter.2.cloned.1.call-start = ((), (), s32[]{:S(2)}) async-start(), calls=%async_computation.5 | async-start | bytes 1671168 | tf_op jit(solution)/shard_map/reduce_scatter | solution.py:70
Sparse Core Ops, SparseCore 0:
  472.6 89.6 reduce-scatter.1
where the time goes:
time: 772 us; the launch traced here: 771 us
  waiting for transfers between devices  592 us (77%)
  local copies, waits for them, and re-layouts  104 us (13%)
  starting transfers between devices  38.1 us (5%)
  between operations  14.3 us (2%)
  matrix products  12.3 us (2%)
  other arithmetic  10.2 us (1%)
    all_to_all x1, waiting for transfers between devices, shards(): lax.all_to_all(sent_rows, 'label', split_axis=0, concat_axis=0, tiled=True)  280 us
    all_to_all x1, waiting for transfers between devices, shards(): lax.all_to_all(slot_grads, 'label', split_axis=0, concat_axis=0, tiled=True)  175 us
    reduce_scatter x1, waiting for transfers between devices, shards(): lax.psum_scatter(local_weight.astype(jnp.bfloat16), 'inst', scatter_dimen...  89.8 us
    all_to_all x1, waiting for transfers between devices, shards(): lax.all_to_all(logit_grad, 'label', split_axis=0, concat_axis=0, tiled=True)  47.3 us
    gather x1, local copies, waits for them, and re-layouts, shards(): padded_codes[bucket_table].astype(jnp.bfloat16)  23 us
    gather x1, local copies, waits for them, and re-layouts, shards(): pair_rows[bucket_table]  23 us
    gather x1, local copies, waits for them, and re-layouts, shards(): padded_rows[pair_rows[bucket_table]]  17.8 us
  transfers between devices with their start and end apart: 5, of which 4 were waited for; matrix products, arithmetic and copies ran while one was open for 8% of the time, Pallas kernels for 0%

commit v1 on v0

v1 whole, which is shorter than its diff:
```python
import functools

import jax
import jax.numpy as jnp
from jax import lax
from jax.experimental import pallas as pl
from jax.experimental.pallas import tpu as pltpu
from jax.sharding import Mesh
from jax.sharding import PartitionSpec as P

BS = 128
MOST = 16
TOP = 16
ROWS = 128
META = 16
D = 768
Z = 16
HALF = BS // 2
COLS = Z * HALF
STEP = 4
PLANE = ("y", "x")
NT = (((1,), (1,)), ((), ()))
F32 = jnp.float32
BF16 = jnp.bfloat16


def expert_body(first, meta, x_ref, w_ref, wt_ref, *refs):
    if first:
        out_ref, gw_ref, acc, grad = refs
    else:
        gw_in, out_ref, gw_ref, acc, grad = refs
    step = pl.program_id(0)
    base = meta[0].astype(F32)
    offset = (meta[1] * HALF + 2).astype(F32)
    n = STEP * ROWS
    x = x_ref[:, :ROWS, :].reshape(n, D)

    @pl.when(step == 0)
    def _():
        if first:
            acc[...] = jnp.zeros_like(acc)
        else:
            acc[...] = gw_in[...]

    wanted = lax.broadcasted_iota(jnp.int32, (Z, ROWS), 0).astype(F32) * 16.0 + base
    before = (
        lax.broadcasted_iota(jnp.int32, (ROWS, ROWS), 0)
        < lax.broadcasted_iota(jnp.int32, (ROWS, ROWS), 1)
    ).astype(F32).astype(BF16)
    entries, ranks = [], []
    for d in range(STEP):
        ids = x_ref[d, ROWS : ROWS + TOP, :ROWS].astype(F32)
        codes = x_ref[d, ROWS : ROWS + TOP, ROWS : 2 * ROWS].astype(F32)
        entry = jnp.zeros((Z, ROWS), F32)
        for k in range(TOP):
            entry = entry + jnp.where(ids[k : k + 1, :] == wanted, codes[k : k + 1, :], 0.0)
        named = entry > 0.0
        rank = jnp.dot(
            jnp.where(named, 1.0, 0.0).astype(BF16), before, preferred_element_type=F32
        )
        entries.append(entry)
        ranks.append(jnp.where(named, rank, -1.0))
    entry = jnp.concatenate(entries, axis=1)
    place = lax.broadcasted_iota(jnp.int32, (HALF, n), 0).astype(F32) + offset
    part = 4 * HALF
    for q in range(COLS // part):
        logits = lax.dot_general(
            w_ref[q * part : (q + 1) * part, :], x, NT, preferred_element_type=F32
        )
        for s in range(4):
            z = 4 * q + s
            code = jnp.broadcast_to(entry[z : z + 1, :], (HALF, n))
            own = logits[s * HALF : (s + 1) * HALF, :]
            sig = 0.5 * jnp.tanh(0.5 * own) + 0.5
            value = jnp.where(code >= 2.0, jnp.where(code == place, sig - 1.0, sig), 0.0)
            grad[z * HALF : (z + 1) * HALF, :] = value.astype(BF16)
    for q in range(COLS // part):
        acc[q * part : (q + 1) * part, :] += jnp.dot(
            grad[q * part : (q + 1) * part, :], x, preferred_element_type=F32
        )
    for q in range(D // 256):
        back = jnp.dot(
            wt_ref[q * 256 : (q + 1) * 256, :], grad[...], preferred_element_type=F32
        ).astype(BF16)
        for d in range(STEP):
            out_ref[d, q * 256 : (q + 1) * 256, :] = back[:, d * ROWS : (d + 1) * ROWS]
    slot = lax.broadcasted_iota(jnp.int32, (MOST, ROWS), 0).astype(F32)
    lane = lax.broadcasted_iota(jnp.int32, (HALF, ROWS), 1) // MOST
    for d in range(STEP):
        for hh in range(2):
            pick = jnp.concatenate(
                [
                    jnp.where(
                        jnp.broadcast_to(ranks[d][z : z + 1, :], (MOST, ROWS)) == slot, 1.0, 0.0
                    )
                    for z in range(8 * hh, 8 * hh + 8)
                ],
                axis=0,
            ).astype(BF16)
            mixed = lax.dot_general(
                grad[hh * 512 : (hh + 1) * 512, d * ROWS : (d + 1) * ROWS],
                pick,
                NT,
                preferred_element_type=F32,
            )
            packed = jnp.zeros((HALF, ROWS), F32)
            for z in range(8):
                packed = jnp.where(lane == z, mixed[z * HALF : (z + 1) * HALF, :], packed)
            out_ref[d, D + hh * HALF : D + (hh + 1) * HALF, :] = packed.astype(BF16)

    @pl.when(step == pl.num_programs(0) - 1)
    def _():
        gw_ref[...] = acc[...].astype(gw_ref.dtype)


def expert(meta, rows, w, wt, total=None):
    first = total is None
    count = rows.shape[0]
    whole = lambda shape: pl.BlockSpec(shape, lambda i, m: (0,) * len(shape))
    in_specs = [
        pl.BlockSpec((STEP, ROWS + META, D), lambda i, m: (i, 0, 0)),
        whole((COLS, D)),
        whole((D, COLS)),
    ]
    args = [meta, rows, w, wt]
    if not first:
        in_specs.append(whole((COLS, D)))
        args.append(total)
    flops = 3 * 2 * count * ROWS * COLS * D
    return pl.pallas_call(
        functools.partial(expert_body, first),
        grid_spec=pltpu.PrefetchScalarGridSpec(
            num_scalar_prefetch=1,
            grid=(count // STEP,),
            in_specs=in_specs,
            out_specs=[
                pl.BlockSpec((STEP, D + BS, ROWS), lambda i, m: (i, 0, 0)),
                whole((COLS, D)),
            ],
            scratch_shapes=[
                pltpu.VMEM((COLS, D), F32),
                pltpu.VMEM((COLS, STEP * ROWS), BF16),
            ],
        ),
        out_shape=[
            jax.ShapeDtypeStruct((count, D + BS, ROWS), BF16),
            jax.ShapeDtypeStruct((COLS, D), F32 if first else BF16),
        ],
        compiler_params=pltpu.CompilerParams(vmem_limit_bytes=48 * 2**20),
        cost_estimate=pl.CostEstimate(
            flops=flops, bytes_accessed=20 * 2**20, transcendentals=count * ROWS * COLS
        ),
    )(*args)


def unpack_body(key_ref, got_ref, out_ref):
    key = key_ref[...]
    lane = lax.broadcasted_iota(jnp.int32, (1, 2 * ROWS), 1)
    total = jnp.zeros(out_ref.shape, F32)
    for owner in range(8):
        for other in range(2):
            chunk = owner * 2 + other
            base = D + other * BS
            table = jnp.concatenate(
                [
                    jnp.concatenate(
                        [
                            got_ref[2 * owner + h, base + hh * HALF : base + (hh + 1) * HALF, :]
                            for hh in range(2)
                        ],
                        axis=1,
                    )
                    for h in range(2)
                ],
                axis=0,
            )
            pick = jnp.where(key == lane + chunk * 2 * ROWS, 1.0, 0.0).astype(BF16)
            total += lax.dot_general(pick, table, NT, preferred_element_type=F32)
    out_ref[...] = total.astype(BF16)


def unpack(key, got):
    pairs = key.shape[0]
    block = 512
    return pl.pallas_call(
        unpack_body,
        grid=(pairs // block,),
        in_specs=[
            pl.BlockSpec((block, 2 * ROWS), lambda i: (i, 0)),
            pl.BlockSpec(got.shape, lambda i: (0, 0, 0)),
        ],
        out_specs=pl.BlockSpec((block, BS), lambda i: (i, 0)),
        out_shape=jax.ShapeDtypeStruct((pairs, BS), BF16),
        compiler_params=pltpu.CompilerParams(vmem_limit_bytes=48 * 2**20),
        cost_estimate=pl.CostEstimate(
            flops=2 * pairs * 4096 * BS, bytes_accessed=8 * 2**20, transcendentals=0
        ),
    )(key, got)


def shards(features, weights, block_ids, label_codes, counts):
    inst = lax.axis_index(PLANE)
    core = lax.axis_index("core")
    meta = jnp.stack([8 * core + inst // 2, inst % 2]).astype(jnp.int32)
    mine = lax.dynamic_slice_in_dim(weights, inst * HALF, HALF, 0)
    w = lax.all_gather(mine, "z").reshape(COLS, D)
    wt = w.T

    alive = jnp.arange(TOP, dtype=jnp.int32)[None, :] < counts[:, None]
    code = jnp.where(alive, jnp.minimum(label_codes, BS) + 2, 1)
    slots = jnp.concatenate([block_ids.T, code.T], axis=1).astype(BF16)
    slots = jnp.pad(slots, ((0, 0), (0, D - 2 * ROWS)))
    sent = jnp.concatenate([features, slots], axis=0)
    own = lax.all_gather(sent, PLANE)
    swap = [(0, 1), (1, 0)]
    other = lax.ppermute(own, "core", swap)
    own_out, total = expert(meta, own, w, wt)
    other_out, total = expert(meta, other, w, wt, total)
    back = lax.ppermute(other_out, "core", swap)
    grad_w = lax.psum_scatter(
        total.reshape(Z, HALF, D), "z", scatter_dimension=0, tiled=False
    ).astype(F32)
    sums = (own_out[:, :D].astype(F32) + back[:, :D].astype(F32)).astype(BF16)
    payload = jnp.concatenate([sums, own_out[:, D:], back[:, D:]], axis=1)
    got = lax.all_to_all(payload, PLANE, split_axis=0, concat_axis=0, tiled=True)
    grad_x = jnp.sum(got[:, :D], axis=0, dtype=F32).T.astype(BF16)

    blocks = jnp.arange(256, dtype=jnp.int32)
    named = (block_ids[:, :, None] == blocks).any(axis=1).astype(BF16)
    order = jnp.arange(ROWS, dtype=jnp.int32)
    before = (order[None, :] < order[:, None]).astype(BF16)
    rank = jnp.dot(before, named, preferred_element_type=F32)
    rank = jnp.sum(jnp.where(block_ids[:, :, None] == blocks, rank[:, None, :], 0.0), axis=2)
    rank = rank.astype(jnp.int32)
    row = block_ids // 16
    owner = block_ids % 16
    crossed = (owner // 8) ^ core
    key = (((owner % 8) * 2 + crossed) * 2 + row // 8) * ROWS + (row % 8) * MOST + rank
    key = jnp.broadcast_to(key.reshape(-1, 1), (ROWS * TOP, 2 * ROWS))
    grad_logits = unpack(key, got).reshape(ROWS, TOP, BS)
    return (grad_x, grad_w, grad_logits)


def solution(mesh):
    mesh = Mesh(mesh.devices.reshape(4, 4, Z, 2), ("y", "x", "z", "core"))
    everywhere = ("y", "x", "z", "core")
    in_specs = (
        P(everywhere, None),
        P(("z", "core"), None),
        P(everywhere, None),
        P(everywhere, None),
        P(everywhere),
    )
    out_specs = (
        P(everywhere, None),
        P(("z", "core", "y", "x"), None),
        P(everywhere, None, None),
    )
    return jax.shard_map(shards, mesh=mesh, in_specs=in_specs, out_specs=out_specs, check_vma=False)
```

time: 772 us -> 303 us (0.39)
  the two profiles are of different devices: /device:TPU:34 before, /device:TPU:2 now
where the time goes in v1:
time: 303 us
  waiting for transfers between devices  217 us (72%)
  Pallas kernels  42.2 us (14%)
  between operations  13.9 us (5%)
  other arithmetic  11.6 us (4%)
  starting transfers between devices  11.3 us (4%)
  local copies, waits for them, and re-layouts  6.16 us (2%)
    all_gather x1, waiting for transfers between devices, shards(): w = lax.all_gather(mine, 'z').reshape(COLS, D)  72.7 us
    reduce_scatter x1, waiting for transfers between devices, shards(): lax.psum_scatter(total.reshape(Z, HALF, D), 'z', scatter_dimension=0, til...  69.6 us
    all_gather x1, waiting for transfers between devices, shards(): own = lax.all_gather(sent, PLANE)  67.9 us
    pallas_call x2, Pallas kernels, expert(): pl.pallas_call(functools.partial(expert_body, first), grid_spec=pltpu.Pre...  34.3 us
    pallas_call x1, Pallas kernels, unpack(): pl.pallas_call(unpack_body, grid=(pairs // block,), in_specs=[pl.BlockSpe...  7.88 us
    all_to_all x1, starting transfers between devices, shards(): lax.all_to_all(payload, PLANE, split_axis=0, concat_axis=0, tiled=True)  7.41 us
    ppermute x1, waiting for transfers between devices, shards(): back = lax.ppermute(other_out, 'core', swap)  6.53 us
  transfers between devices with their start and end apart: 6, of which 4 were waited for; matrix products, arithmetic and copies ran while one was open for 2% of the time, Pallas kernels for 6%

profile of v1, /device:TPU:2, one launch (start us, length us, event | category | flops | bytes accessed | tf_op | source)
XLA Modules:
  0.0 302.8 jit_solution(6231334232628049773)
XLA Ops:
  7.2 0.0 copy-start
  7.2 0.0 all-gather.5.cloned.1.call-start
  7.2 0.9 copy.31
  8.1 0.7 fusion.23
  8.9 0.1 copy.32
  8.9 0.7 convert_bitcast_fusion
  9.7 1.6 pad_maximum_fusion.1
  11.3 0.0 all-gather.5.cloned.1.call-update
  11.3 0.0 all-gather.7.cloned.1.call-start
  11.4 0.0 copy-done
  11.4 0.7 constant_dynamic-slice_fusion
  12.0 0.0 all-gather.7.cloned.1.call-update
  12.1 67.9 %all-gather.5.cloned.1.call-done = bf16[2304,768]{1,0:T(8,128)(2,1)} async-done(((bf16[144,768]{1,0:T(8,128)(2,1)}), bf16[2304,768]{1,0:T(8,128)(2,1)}) %all-gather.5.cloned.1.call-update) | async-done | bytes 3538960 | tf_op jit(solution)/shard_map/all_gather | solution.py:214
  80.0 1.9 collective-permute-start
  81.9 0.1 pad_add_fusion.meta
  82.0 72.7 %all-gather.7.cloned.1.call-done.w_ref = bf16[1024,768]{1,0:T(8,128)(2,1)} async-done(((bf16[64,768]{1,0:T(8,128)(2,1)}), bf16[1024,768]{1,0:T(8,128)(2,1)}) %all-gather.7.cloned.1.call-update) | async-done | bytes 1572880 | tf_op jit(solution)/shard_map/all_gather | solution.py:206
  154.7 1.7 copy.33
  156.4 0.0 copy-start.1
  156.4 1.4 copy-done.1
  157.8 0.0 copy-start.2
  157.8 16.8 %shard_map.76 = (bf16[16,896,128]{2,1,0:T(8,128)(2,1)}, f32[1024,768]{1,0:T(8,128)}) custom-call(s32[2]{0:T(128)S(1)} %pad_add_fusion.meta, bf16[16,144,768]{2,1,0:T(8,128)(2,1)} %bitcast.19, bf16[1024,768]{1,0:T(8,128)(2,1)S(1)} %copy-done.1, bf16[768,1024]{1,0:T(8,128)(2,1)S(1)} %bitcast.15), custom_call_target="tpu_custom_call" | custom-call | flops 9663676416 | bytes 20971520 | tf_op jit(solution)/shard_map/pallas_call | solution.py:130
  174.7 0.0 collective-permute-done.x_ref
  174.7 0.0 copy-done.2
  174.7 0.0 copy-start.3
  174.7 17.5 %shard_map.77 = (bf16[16,896,128]{2,1,0:T(8,128)(2,1)}, bf16[1024,768]{1,0:T(8,128)(2,1)}) custom-call(s32[2]{0:T(128)S(1)} %pad_add_fusion.meta, bf16[16,144,768]{2,1,0:T(8,128)(2,1)} %collective-permute-done.x_ref, bf16[1024,768]{1,0:T(8,128)(2,1)S(1)} %copy-done.2, bf16[768,1024]{1,0:T(8,128)(2,1)S(1)} %bitcast.16, f32[1024,768]{1,0:T(8,128)} %get-tuple-element.8.refs_0_), custom_call_target="tpu_custom_call" | custom-call | flops 9663676416 | bytes 20971520 | tf_op jit(solution)/shard_map/pallas_call | solution.py:130
  192.2 1.9 collective-permute-start.1
  194.1 0.0 copy-done.3
  194.2 6.5 %collective-permute-done.1 = bf16[16,896,128]{2,1,0:T(8,128)(2,1)S(1)} collective-permute-done((bf16[16,896,128]{2,1,0:T(8,128)(2,1)}, bf16[16,896,128]{2,1,0:T(8,128)(2,1)S(1)}, u32[]{:S(2)}, u32[]{:S(2)}) %collective-permute-start.1) | collective-permute-done | bytes 3670048 | tf_op jit(solution)/shard_map/ppermute | solution.py:219
  200.7 0.8 add_convert_fusion
  201.6 2.2 pad_maximum_fusion
  203.7 0.0 copy-start.4
  203.7 7.4 %all-to-all-start = ((bf16[16,1024,128]{2,1,0:T(8,128)(2,1)}), bf16[16,1024,128]{2,1,0:T(8,128)(2,1)}, u32[]{:S(2)}, u32[]{:S(2)}) async-start(bf16[16,1024,128]{2,1,0:T(8,128)(2,1)} %pad_maximum_fusion), calls=%async_computation | async-start | bytes 8388608 | tf_op jit(solution)/shard_map/all_to_all | solution.py:225
  211.1 0.0 reduce-scatter.2.cloned.1.call-start
  211.2 0.7 reduce-scatter.2.cloned.1.call-update
  211.9 0.0 copy-done.4
  211.9 0.1 copy.34
  212.0 0.6 fusion
  212.6 0.2 fusion.19
  212.7 0.7 select_reduce_fusion
  213.5 0.2 fusion.7
  213.7 0.1 broadcast_in_dim.35
  213.8 69.6 %reduce-scatter.2.cloned.1.call-done = bf16[1,64,768]{2,1,0:T(8,128)(2,1)} async-done(((bf16[16,64,768]{2,1,0:T(8,128)(2,1)}), bf16[1,64,768]{2,1,0:T(8,128)(2,1)}) %reduce-scatter.2.cloned.1.call-update) | async-done | bytes 98320 | tf_op jit(solution)/shard_map/reduce_scatter | solution.py:220
  283.3 1.6 bitcast_convert_fusion
  284.9 0.0 all-to-all-done.got_ref
  284.9 2.3 slice_reduce_fusion
  287.2 0.8 copy.39
  288.1 0.3 broadcast_in_dim.36.key_ref
  288.4 7.9 %shard_map.78 = bf16[2048,128]{1,0:T(8,128)(2,1)} custom-call(s32[2048,256]{1,0:T(8,128)S(1)} %broadcast_in_dim.36.key_ref, bf16[16,1024,128]{2,1,0:T(8,128)(2,1)} %all-to-all-done.got_ref), custom_call_target="tpu_custom_call" | custom-call | flops 2147483648 | bytes 8388608 | tf_op jit(solution)/shard_map/pallas_call | solution.py:185
  (3 shorter events, 0.1 us)
Async XLA Ops:
  7.2 4.2 %copy-start = (bf16[1024,768]{1,0:T(8,128)(2,1)S(1)}, bf16[1024,768]{1,0:T(8,128)(2,1)}, u32[]{:S(2)}) copy-start(bf16[1024,768]{1,0:T(8,128)(2,1)} %param.6) | copy-start | bytes 4718596
  7.2 72.8 %all-gather.5.cloned.1.call-start = ((), (), s32[]{:S(2)}) async-start(), calls=%async_computation.3 | async-start | bytes 3760128 | tf_op jit(solution)/shard_map/all_gather | solution.py:214
  11.3 143.4 %all-gather.7.cloned.1.call-start = ((), (), s32[]{:S(2)}) async-start(), calls=%async_computation.4 | async-start | bytes 1671168 | tf_op jit(solution)/shard_map/all_gather | solution.py:206
  80.0 94.7 %collective-permute-start = (bf16[16,144,768]{2,1,0:T(8,128)(2,1)}, bf16[16,144,768]{2,1,0:T(8,128)(2,1)}, u32[]{:S(2)}, u32[]{:S(2)}) collective-permute-start(bf16[16,144,768]{2,1,0:T(8,128)(2,1)} %bitcast.18), channel_id=1, source_target_pairs={{0,1},{1,0},{2,3},{3,2},{4,5},{5,4},{6,7},{7,6},{8,9},{9,8},{10,11... | collective-permute-start | bytes 10616840 | tf_op jit(solution)/shard_map/ppermute | solution.py:216
  156.4 1.4 copy-start.1
  157.8 16.9 %copy-start.2 = (bf16[1024,768]{1,0:T(8,128)(2,1)S(1)}, bf16[1024,768]{1,0:T(8,128)(2,1)}, u32[]{:S(2)}) copy-start(bf16[1024,768]{1,0:T(8,128)(2,1)} %all-gather.7.cloned.1.call-done.w_ref) | copy-start | bytes 4718596
  174.7 19.4 %copy-start.3 = (bf16[16,896,128]{2,1,0:T(8,128)(2,1)S(1)}, bf16[16,896,128]{2,1,0:T(8,128)(2,1)}, u32[]{:S(2)}) copy-start(bf16[16,896,128]{2,1,0:T(8,128)(2,1)} %get-tuple-element.7) | copy-start | bytes 11010052
  192.2 8.5 %collective-permute-start.1 = (bf16[16,896,128]{2,1,0:T(8,128)(2,1)}, bf16[16,896,128]{2,1,0:T(8,128)(2,1)S(1)}, u32[]{:S(2)}, u32[]{:S(2)}) collective-permute-start(bf16[16,896,128]{2,1,0:T(8,128)(2,1)} %get-tuple-element.9), channel_id=1, source_target_pairs={{0,1},{1,0},{2,3},{3,2},{4,5},{5,4},{6,7},{7,6},{8,9},{9,8},{10,11... | collective-permute-start | bytes 11010056 | tf_op jit(solution)/shard_map/ppermute | solution.py:219
  203.7 8.1 %copy-start.4 = (s32[128,16]{0,1:T(8,128)S(1)}, s32[128,16]{0,1:T(8,128)}, u32[]{:S(2)}) copy-start(s32[128,16]{0,1:T(8,128)} %param.7) | copy-start | bytes 24580
  203.7 81.2 %all-to-all-start = ((bf16[16,1024,128]{2,1,0:T(8,128)(2,1)}), bf16[16,1024,128]{2,1,0:T(8,128)(2,1)}, u32[]{:S(2)}, u32[]{:S(2)}) async-start(bf16[16,1024,128]{2,1,0:T(8,128)(2,1)} %pad_maximum_fusion), calls=%async_computation | async-start | bytes 8388608 | tf_op jit(solution)/shard_map/all_to_all | solution.py:225
  211.1 72.2 %reduce-scatter.2.cloned.1.call-start = ((), (), s32[]{:S(2)}) async-start(), calls=%async_computation.2 | async-start | bytes 1671168 | tf_op jit(solution)/shard_map/reduce_scatter | solution.py:220
Sparse Core Ops, SparseCore 0:
  11.6 68.3 all-gather.4
  82.6 72.0 all-gather.6
  214.8 68.4 reduce-scatter.1

commit v2 on v1

--- a/solution.py
+++ b/solution.py
@@ -22,27 +22,16 @@
 NT = (((1,), (1,)), ((), ()))
 F32 = jnp.float32
 BF16 = jnp.bfloat16
-
-
-def expert_body(first, meta, x_ref, w_ref, wt_ref, *refs):
-    if first:
-        out_ref, gw_ref, acc, grad = refs
-    else:
-        gw_in, out_ref, gw_ref, acc, grad = refs
-    step = pl.program_id(0)
+VMEM = 48 * 2**20
+
+
+def expert_body(meta, x_ref, w_ref, grad, pack_ref):
     base = meta[0].astype(F32)
     offset = (meta[1] * HALF + 2).astype(F32)
     n = STEP * ROWS
     x = x_ref[:, :ROWS, :].reshape(n, D)
-
-    @pl.when(step == 0)
-    def _():
-        if first:
-            acc[...] = jnp.zeros_like(acc)
-        else:
-            acc[...] = gw_in[...]
-
-    wanted = lax.broadcasted_iota(jnp.int32, (Z, ROWS), 0).astype(F32) * 16.0 + base
+    chunk = lax.rem(lax.broadcasted_iota(jnp.int32, (Z, ROWS), 0) + meta[2], Z)
+    wanted = chunk.astype(F32) * 16.0 + base
     before = (
         lax.broadcasted_iota(jnp.int32, (ROWS, ROWS), 0)
         < lax.broadcasted_iota(jnp.int32, (ROWS, ROWS), 1)
@@ -74,16 +63,6 @@
             sig = 0.5 * jnp.tanh(0.5 * own) + 0.5
             value = jnp.where(code >= 2.0, jnp.where(code == place, sig - 1.0, sig), 0.0)
             grad[z * HALF : (z + 1) * HALF, :] = value.astype(BF16)
-    for q in range(COLS // part):
-        acc[q * part : (q + 1) * part, :] += jnp.dot(
-            grad[q * part : (q + 1) * part, :], x, preferred_element_type=F32
-        )
-    for q in range(D // 256):
-        back = jnp.dot(
-            wt_ref[q * 256 : (q + 1) * 256, :], grad[...], preferred_element_type=F32
-        ).astype(BF16)
-        for d in range(STEP):
-            out_ref[d, q * 256 : (q + 1) * 256, :] = back[:, d * ROWS : (d + 1) * ROWS]
     slot = lax.broadcasted_iota(jnp.int32, (MOST, ROWS), 0).astype(F32)
     lane = lax.broadcasted_iota(jnp.int32, (HALF, ROWS), 1) // MOST
     for d in range(STEP):
@@ -106,51 +85,142 @@
             packed = jnp.zeros((HALF, ROWS), F32)
             for z in range(8):
                 packed = jnp.where(lane == z, mixed[z * HALF : (z + 1) * HALF, :], packed)
-            out_ref[d, D + hh * HALF : D + (hh + 1) * HALF, :] = packed.astype(BF16)
-
-    @pl.when(step == pl.num_programs(0) - 1)
-    def _():
-        gw_ref[...] = acc[...].astype(gw_ref.dtype)
-
-
-def expert(meta, rows, w, wt, total=None):
-    first = total is None
+            pack_ref[d, hh * HALF : (hh + 1) * HALF, :] = packed.astype(BF16)
+
+
+def expert(meta, rows, w):
     count = rows.shape[0]
-    whole = lambda shape: pl.BlockSpec(shape, lambda i, m: (0,) * len(shape))
-    in_specs = [
-        pl.BlockSpec((STEP, ROWS + META, D), lambda i, m: (i, 0, 0)),
-        whole((COLS, D)),
-        whole((D, COLS)),
-    ]
-    args = [meta, rows, w, wt]
-    if not first:
-        in_specs.append(whole((COLS, D)))
-        args.append(total)
-    flops = 3 * 2 * count * ROWS * COLS * D
     return pl.pallas_call(
-        functools.partial(expert_body, first),
+        expert_body,
         grid_spec=pltpu.PrefetchScalarGridSpec(
             num_scalar_prefetch=1,
             grid=(count // STEP,),
-            in_specs=in_specs,
+            in_specs=[
+                pl.BlockSpec((STEP, ROWS + META, D), lambda i, m: (i, 0, 0)),
+                pl.BlockSpec((COLS, D), lambda i, m: (0, 0)),
+            ],
             out_specs=[
-                pl.BlockSpec((STEP, D + BS, ROWS), lambda i, m: (i, 0, 0)),
-                whole((COLS, D)),
+                pl.BlockSpec((COLS, STEP * ROWS), lambda i, m: (0, i)),
+                pl.BlockSpec((STEP, BS, ROWS), lambda i, m: (i, 0, 0)),
             ],
-            scratch_shapes=[
-                pltpu.VMEM((COLS, D), F32),
-                pltpu.VMEM((COLS, STEP * ROWS), BF16),
-            ],
         ),
         out_shape=[
-            jax.ShapeDtypeStruct((count, D + BS, ROWS), BF16),
-            jax.ShapeDtypeStruct((COLS, D), F32 if first else BF16),
+            jax.ShapeDtypeStruct((COLS, count * ROWS), BF16),
+            jax.ShapeDtypeStruct((count, BS, ROWS), BF16),
         ],
-        compiler_params=pltpu.CompilerParams(vmem_limit_bytes=48 * 2**20),
+        compiler_params=pltpu.CompilerParams(vmem_limit_bytes=VMEM),
         cost_estimate=pl.CostEstimate(
-            flops=flops, bytes_accessed=20 * 2**20, transcendentals=count * ROWS * COLS
-        ),
-    )(*args)
+            flops=2 * count * ROWS * COLS * D,
+            bytes_accessed=10 * 2**20,
+            transcendentals=count * ROWS * COLS,
+        ),
+    )(meta, rows, w)
+
+
+def weight_body(ga_ref, xa_ref, gb_ref, xb_ref, out_ref, acc):
+    step, half = pl.program_id(0), pl.num_programs(0) // 2
+
+    def add(g_ref, x_ref):
+        x = x_ref[:, :ROWS, :].reshape(-1, D)
+        for q in range(4):
+            rows = slice(q * 256, (q + 1) * 256)
+            acc[rows, :] += jnp.dot(g_ref[rows, :], x, preferred_element_type=F32)
+
+    @pl.when(step == 0)
+    def _():
+        acc[...] = jnp.zeros_like(acc)
+
+    @pl.when(step < half)
+    def _():
+        add(ga_ref, xa_ref)
+
+    @pl.when(step >= half)
+    def _():
+        add(gb_ref, xb_ref)
+
+    @pl.when(step == pl.num_programs(0) - 1)
+    def _():
+        out_ref[...] = acc[...].astype(BF16)
+
+
+def weight_grad(ga, xa, gb, xb):
+    count, block = xa.shape[0], 8
+    half = count // block
+    low = lambda i: jnp.minimum(i, half - 1)
+    high = lambda i: jnp.maximum(i - half, 0)
+    return pl.pallas_call(
+        weight_body,
+        grid=(2 * half,),
+        in_specs=[
+            pl.BlockSpec((COLS, block * ROWS), lambda i: (0, low(i))),
+            pl.BlockSpec((block, ROWS + META, D), lambda i: (low(i), 0, 0)),
+            pl.BlockSpec((COLS, block * ROWS), lambda i: (0, high(i))),
+            pl.BlockSpec((block, ROWS + META, D), lambda i: (high(i), 0, 0)),
+        ],
+        out_specs=pl.BlockSpec((COLS, D), lambda i: (0, 0)),
+        out_shape=jax.ShapeDtypeStruct((COLS, D), BF16),
+        scratch_shapes=[pltpu.VMEM((COLS, D), F32)],
+        compiler_params=pltpu.CompilerParams(vmem_limit_bytes=VMEM),
+        cost_estimate=pl.CostEstimate(
+            flops=4 * count * ROWS * COLS * D, bytes_accessed=18 * 2**20, transcendentals=0
+        ),
+    )(ga, xa, gb, xb)
+
+
+def row_body(wt_ref, g_ref, out_ref):
+    for q in range(D // 256):
+        back = jnp.dot(
+            wt_ref[q * 256 : (q + 1) * 256, :], g_ref[...], preferred_element_type=F32
+        ).astype(BF16)
+        for d in range(STEP):
+            out_ref[d, q * 256 : (q + 1) * 256, :] = back[:, d * ROWS : (d + 1) * ROWS]
+
+
+def row_grad(wt, g):
+    count = g.shape[1] // ROWS
+    return pl.pallas_call(
+        row_body,
+        grid=(count // STEP,),
+        in_specs=[
+            pl.BlockSpec((D, COLS), lambda i: (0, 0)),
+            pl.BlockSpec((COLS, STEP * ROWS), lambda i: (0, i)),
+        ],
+        out_specs=pl.BlockSpec((STEP, D, ROWS), lambda i: (i, 0, 0)),
+        out_shape=jax.ShapeDtypeStruct((count, D, ROWS), BF16),
+        compiler_params=pltpu.CompilerParams(vmem_limit_bytes=VMEM),
+        cost_estimate=pl.CostEstimate(
+            flops=2 * count * ROWS * COLS * D, bytes_accessed=9 * 2**20, transcendentals=0
+        ),
+    )(wt, g)
+
+
+def shift(x, k):
+    return lax.ppermute(x, "z", [(s, (s - k) % Z) for s in range(Z)])
+
+
+def gather_z(mine):
+    ahead, behind, across = shift(mine, 4), shift(mine, -4), shift(mine, 8)
+    every = jnp.stack([mine, ahead, across, behind])
+    half = HALF // 2
+    one, last = shift(every, 1), shift(every, -1)
+    low, high = shift(every[:, :half], 2), shift(every[:, half:], -2)
+    two = jnp.concatenate([low, jnp.roll(high, -1, axis=0)], axis=1)
+    parts = [every, one, two, jnp.roll(last, -1, axis=0)]
+    return jnp.stack(parts, axis=1).reshape((Z,) + mine.shape)
+
+
+def reduce_z(total):
+    half = HALF // 2
+    total = total.reshape(4, 4, HALF, D)
+    last = jnp.roll(total[:, 3], 1, axis=0)
+    two = total[:, 2]
+    one, last = shift(total[:, 1], -1), shift(last, 1)
+    low, high = shift(two[:, :half], -2), shift(jnp.roll(two[:, half:], 1, axis=0), 2)
+    every = total[:, 0].astype(F32) + one.astype(F32) + last.astype(F32)
+    every = every + jnp.concatenate([low, high], axis=1).astype(F32)
+    sent = every[1:].astype(BF16)
+    got = [shift(sent[0], -4), shift(sent[1], 8), shift(sent[2], 4)]
+    return every[0] + got[0].astype(F32) + got[1].astype(F32) + got[2].astype(F32)
 
 
 def unpack_body(key_ref, got_ref, out_ref):
@@ -160,7 +230,7 @@
     for owner in range(8):
         for other in range(2):
             chunk = owner * 2 + other
-            base = D + other * BS
+            base = other * BS
             table = jnp.concatenate(
                 [
                     jnp.concatenate(
@@ -191,7 +261,7 @@
         ],
         out_specs=pl.BlockSpec((block, BS), lambda i: (i, 0)),
         out_shape=jax.ShapeDtypeStruct((pairs, BS), BF16),
-        compiler_params=pltpu.CompilerParams(vmem_limit_bytes=48 * 2**20),
+        compiler_params=pltpu.CompilerParams(vmem_limit_bytes=VMEM),
         cost_estimate=pl.CostEstimate(
             flops=2 * pairs * 4096 * BS, bytes_accessed=8 * 2**20, transcendentals=0
         ),
@@ -201,9 +271,10 @@
 def shards(features, weights, block_ids, label_codes, counts):
     inst = lax.axis_index(PLANE)
     core = lax.axis_index("core")
-    meta = jnp.stack([8 * core + inst // 2, inst % 2]).astype(jnp.int32)
+    depth = lax.axis_index("z")
+    meta = jnp.stack([8 * core + inst // 2, inst % 2, depth]).astype(jnp.int32)
     mine = lax.dynamic_slice_in_dim(weights, inst * HALF, HALF, 0)
-    w = lax.all_gather(mine, "z").reshape(COLS, D)
+    w = gather_z(mine).reshape(COLS, D)
     wt = w.T
 
     alive = jnp.arange(TOP, dtype=jnp.int32)[None, :] < counts[:, None]
@@ -211,19 +282,22 @@
     slots = jnp.concatenate([block_ids.T, code.T], axis=1).astype(BF16)
     slots = jnp.pad(slots, ((0, 0), (0, D - 2 * ROWS)))
     sent = jnp.concatenate([features, slots], axis=0)
-    own = lax.all_gather(sent, PLANE)
+    copies = jnp.broadcast_to(sent[None], (Z,) + sent.shape)
+    own = lax.all_to_all(copies, PLANE, split_axis=0, concat_axis=0, tiled=True)
     swap = [(0, 1), (1, 0)]
     other = lax.ppermute(own, "core", swap)
-    own_out, total = expert(meta, own, w, wt)
-    other_out, total = expert(meta, other, w, wt, total)
-    back = lax.ppermute(other_out, "core", swap)
-    grad_w = lax.psum_scatter(
-        total.reshape(Z, HALF, D), "z", scatter_dimension=0, tiled=False
-    ).astype(F32)
-    sums = (own_out[:, :D].astype(F32) + back[:, :D].astype(F32)).astype(BF16)
-    payload = jnp.concatenate([sums, own_out[:, D:], back[:, D:]], axis=1)
-    got = lax.all_to_all(payload, PLANE, split_axis=0, concat_axis=0, tiled=True)
-    grad_x = jnp.sum(got[:, :D], axis=0, dtype=F32).T.astype(BF16)
+    own_grad, own_pack = expert(meta, own, w)
+    other_grad, other_pack = expert(meta, other, w)
+    total = weight_grad(own_grad, own, other_grad, other)
+    back_pack = lax.ppermute(other_pack, "core", swap)
+    packs = jnp.concatenate([own_pack, back_pack], axis=1)
+    got = lax.all_to_all(packs, PLANE, split_axis=0, concat_axis=0, tiled=True)
+    total, other_grad, own_grad = lax.optimization_barrier((total, other_grad, own_grad))
+    grad_w = reduce_z(total)
+    back_rows = lax.ppermute(row_grad(wt, other_grad), "core", swap)
+    sums = (row_grad(wt, own_grad).astype(F32) + back_rows.astype(F32)).astype(BF16)
+    got_rows = lax.all_to_all(sums, PLANE, split_axis=0, concat_axis=0, tiled=True)
+    grad_x = jnp.sum(got_rows, axis=0, dtype=F32).T.astype(BF16)
 
     blocks = jnp.arange(256, dtype=jnp.int32)
     named = (block_ids[:, :, None] == blocks).any(axis=1).astype(BF16)
@@ -232,7 +306,7 @@
     rank = jnp.dot(before, named, preferred_element_type=F32)
     rank = jnp.sum(jnp.where(block_ids[:, :, None] == blocks, rank[:, None, :], 0.0), axis=2)
     rank = rank.astype(jnp.int32)
-    row = block_ids // 16
+    row = (block_ids // 16 - depth) % Z
     owner = block_ids % 16
     crossed = (owner // 8) ^ core
     key = (((owner % 8) * 2 + crossed) * 2 + row // 8) * ROWS + (row % 8) * MOST + rank

time: 303 us -> 277 us (0.914)
  the two profiles are of different devices: /device:TPU:2 before, /device:TPU:1 now
where the time goes in v2:
time: 277 us; the launch traced here: 276 us
  starting transfers between devices  94 us (34%)
  waiting for transfers between devices  61.6 us (22%)
  blocking collectives  48.6 us (18%)
  Pallas kernels  47.9 us (17%)
  other arithmetic  16.9 us (6%)
  local copies, waits for them, and re-layouts  5.69 us (2%)
    ppermute x14, starting transfers between devices, shift(): return lax.ppermute(x, 'z', [(s, (s - k) % Z) for s in range(Z)])  74.1 us
    ppermute x14, waiting for transfers between devices, shift(): return lax.ppermute(x, 'z', [(s, (s - k) % Z) for s in range(Z)])  50.3 us
    all_to_all x1, blocking collectives, shards(): own = lax.all_to_all(copies, PLANE, split_axis=0, concat_axis=0, tiled=True)  48.6 us
    pallas_call x2, Pallas kernels, expert(): pl.pallas_call(expert_body, grid_spec=pltpu.PrefetchScalarGridSpec(num_sc...  17.5 us
    pallas_call x2, Pallas kernels, row_grad(): pl.pallas_call(row_body, grid=(count // STEP,), in_specs=[pl.BlockSpec((D...  12.2 us
    pallas_call x1, Pallas kernels, weight_grad(): pl.pallas_call(weight_body, grid=(2 * half,), in_specs=[pl.BlockSpec((COL...  11.4 us
    all_to_all x1, waiting for transfers between devices, shards(): got = lax.all_to_all(packs, PLANE, split_axis=0, concat_axis=0, tiled=True)  7.22 us
    pallas_call x1, Pallas kernels, unpack(): pl.pallas_call(unpack_body, grid=(pairs // block,), in_specs=[pl.BlockSpe...  6.91 us
  transfers between devices with their start and end apart: 19, of which 12 were waited for; matrix products, arithmetic and copies ran while one was open for 5% of the time, Pallas kernels for 8%

profile of v2, /device:TPU:1, one launch (start us, length us, event | category | flops | bytes accessed | tf_op | source)
XLA Modules:
  0.0 275.9 jit_solution(14797179241801634261)
XLA Ops:
  0.6 0.9 copy.54
  1.6 0.7 fusion.30
  2.3 0.1 copy.55
  2.4 0.7 convert_bitcast_fusion
  3.1 0.9 pad_maximum_fusion.4
  4.0 0.2 broadcast_in_dim.23
  4.3 48.6 %all_to_all.15.x_ref.xa_ref = bf16[16,144,768]{2,1,0:T(8,128)(2,1)} all-to-all(bf16[16,144,768]{2,1,0:T(8,128)(2,1)S(1)} %broadcast_in_dim.23), channel_id=1, replica_groups=mesh['y'=4,'x'=4,'z'=16,'core'=2] {'y','x'}, dimensions={0} | all-to-all | bytes 7077888 | tf_op jit(solution)/shard_map/all_to_all | solution.py:286
  52.9 5.8 %collective-permute-start.7 = (bf16[16,144,768]{2,1,0:T(8,128)(2,1)}, bf16[16,144,768]{2,1,0:T(8,128)(2,1)}, u32[]{:S(2)}, u32[]{:S(2)}) collective-permute-start(bf16[16,144,768]{2,1,0:T(8,128)(2,1)} %all_to_all.15.x_ref.xa_ref), channel_id=1, source_target_pairs={{0,1},{1,0},{2,3},{3,2},{4,5},{5,4},{6,7},{7,6},{8,9},{9,8},{10,11... | collective-permute-start | bytes 10616840 | tf_op jit(solution)/shard_map/ppermute | solution.py:288
  58.8 12.2 %collective-permute-start = (bf16[64,768]{1,0:T(8,128)(2,1)S(1)}, bf16[64,768]{1,0:T(8,128)(2,1)S(1)}, u32[]{:S(2)}, u32[]{:S(2)}) collective-permute-start(bf16[64,768]{1,0:T(8,128)(2,1)S(1)} %constant_dynamic-slice_fusion), channel_id=1, source_target_pairs={{0,24},{2,26},{4,28},{6,30},{8,0},{10,2},{12,4},{14,6},{16,8},{18,... | collective-permute-start | bytes 294920 | tf_op jit(solution)/shard_map/ppermute | solution.py:198
  71.0 4.9 %collective-permute-start.1 = (bf16[64,768]{1,0:T(8,128)(2,1)S(1)}, bf16[64,768]{1,0:T(8,128)(2,1)S(1)}, u32[]{:S(2)}, u32[]{:S(2)}) collective-permute-start(bf16[64,768]{1,0:T(8,128)(2,1)S(1)} %constant_dynamic-slice_fusion), channel_id=1, source_target_pairs={{0,16},{2,18},{4,20},{6,22},{8,24},{10,26},{12,28},{14,30},{16,0},... | collective-permute-start | bytes 294920 | tf_op jit(solution)/shard_map/ppermute | solution.py:198
  75.9 7.3 %collective-permute-start.2 = (bf16[64,768]{1,0:T(8,128)(2,1)S(1)}, bf16[64,768]{1,0:T(8,128)(2,1)S(1)}, u32[]{:S(2)}, u32[]{:S(2)}) collective-permute-start(bf16[64,768]{1,0:T(8,128)(2,1)S(1)} %constant_dynamic-slice_fusion), channel_id=1, source_target_pairs={{0,8},{2,10},{4,12},{6,14},{8,16},{10,18},{12,20},{14,22},{16,24},... | collective-permute-start | bytes 294920 | tf_op jit(solution)/shard_map/ppermute | solution.py:198
  83.2 2.0 collective-permute-done
  85.2 0.7 collective-permute-done.1
  85.9 3.7 %collective-permute-done.2 = bf16[64,768]{1,0:T(8,128)(2,1)S(1)} collective-permute-done((bf16[64,768]{1,0:T(8,128)(2,1)S(1)}, bf16[64,768]{1,0:T(8,128)(2,1)S(1)}, u32[]{:S(2)}, u32[]{:S(2)}) %collective-permute-start.2) | collective-permute-done | bytes 98336 | tf_op jit(solution)/shard_map/ppermute | solution.py:198
  89.6 0.1 fusion.32
  89.7 6.4 %collective-permute-start.6 = (bf16[4,64,768]{2,1,0:T(8,128)(2,1)S(1)}, bf16[4,64,768]{2,1,0:T(8,128)(2,1)S(1)}, u32[]{:S(2)}, u32[]{:S(2)}) collective-permute-start(bf16[4,64,768]{2,1,0:T(8,128)(2,1)S(1)} %get-tuple-element.34), channel_id=1, source_target_pairs={{0,2},{2,4},{4,6},{6,8},{8,10},{10,12},{12,14},{14,16},{16,18},{18... | collective-permute-start | bytes 1179656 | tf_op jit(solution)/shard_map/ppermute | solution.py:198
  96.1 7.1 %collective-permute-start.5 = (bf16[4,32,768]{2,1,0:T(8,128)(2,1)S(1)}, bf16[4,32,768]{2,1,0:T(8,128)(2,1)S(1)}, u32[]{:S(2)}, u32[]{:S(2)}) collective-permute-start(bf16[4,32,768]{2,1,0:T(8,128)(2,1)S(1)} %get-tuple-element.36), channel_id=1, source_target_pairs={{0,4},{2,6},{4,8},{6,10},{8,12},{10,14},{12,16},{14,18},{16,20},{1... | collective-permute-start | bytes 589832 | tf_op jit(solution)/shard_map/ppermute | solution.py:198
  103.1 4.4 %collective-permute-start.4 = (bf16[4,32,768]{2,1,0:T(8,128)(2,1)S(1)}, bf16[4,32,768]{2,1,0:T(8,128)(2,1)}, u32[]{:S(2)}, u32[]{:S(2)}) collective-permute-start(bf16[4,32,768]{2,1,0:T(8,128)(2,1)S(1)} %get-tuple-element.35), channel_id=1, source_target_pairs={{0,28},{2,30},{4,0},{6,2},{8,4},{10,6},{12,8},{14,10},{16,12},{18,... | collective-permute-start | bytes 589832 | tf_op jit(solution)/shard_map/ppermute | solution.py:198
  107.5 3.1 %collective-permute-start.3 = (bf16[4,64,768]{2,1,0:T(8,128)(2,1)S(1)}, bf16[4,64,768]{2,1,0:T(8,128)(2,1)}, u32[]{:S(2)}, u32[]{:S(2)}) collective-permute-start(bf16[4,64,768]{2,1,0:T(8,128)(2,1)S(1)} %get-tuple-element.34), channel_id=1, source_target_pairs={{0,30},{2,0},{4,2},{6,4},{8,6},{10,8},{12,10},{14,12},{16,14},{18,... | collective-permute-start | bytes 1179656 | tf_op jit(solution)/shard_map/ppermute | solution.py:198
  110.6 0.1 pad_add_fusion.meta
  110.7 10.1 %collective-permute-done.5 = bf16[4,32,768]{2,1,0:T(8,128)(2,1)S(1)} collective-permute-done((bf16[4,32,768]{2,1,0:T(8,128)(2,1)S(1)}, bf16[4,32,768]{2,1,0:T(8,128)(2,1)S(1)}, u32[]{:S(2)}, u32[]{:S(2)}) %collective-permute-start.5) | collective-permute-done | bytes 196640 | tf_op jit(solution)/shard_map/ppermute | solution.py:198
  120.8 1.0 maximum_bitcast_fusion
  121.9 3.0 %collective-permute-done.3 = bf16[4,64,768]{2,1,0:T(8,128)(2,1)} collective-permute-done((bf16[4,64,768]{2,1,0:T(8,128)(2,1)S(1)}, bf16[4,64,768]{2,1,0:T(8,128)(2,1)}, u32[]{:S(2)}, u32[]{:S(2)}) %collective-permute-start.3) | collective-permute-done | bytes 393248 | tf_op jit(solution)/shard_map/ppermute | solution.py:198
  124.9 1.2 pad_maximum_fusion
  126.1 1.6 copy.53
  127.7 8.7 %shard_map.76 = (bf16[1024,2048]{1,0:T(8,128)(2,1)}, bf16[16,128,128]{2,1,0:T(8,128)(2,1)S(1)}) custom-call(s32[3]{0:T(128)S(1)} %pad_add_fusion.meta, bf16[16,144,768]{2,1,0:T(8,128)(2,1)} %all_to_all.15.x_ref.xa_ref, bf16[1024,768]{1,0:T(8,128)(2,1)S(1)} %bitcast.66), custom_call_target="tpu_custom_call" | custom-call | flops 3221225472 | bytes 10485760 | tf_op jit(solution)/shard_map/pallas_call | solution.py:93
  136.4 8.7 %shard_map.77 = (bf16[1024,2048]{1,0:T(8,128)(2,1)}, bf16[16,128,128]{2,1,0:T(8,128)(2,1)S(1)}) custom-call(s32[3]{0:T(128)S(1)} %pad_add_fusion.meta, bf16[16,144,768]{2,1,0:T(8,128)(2,1)} %collective-permute-done.7.x_ref.xb_ref, bf16[1024,768]{1,0:T(8,128)(2,1)S(1)} %bitcast.67), custom_call_target="tpu_custom_call" | custom-call | flops 3221225472 | bytes 10485760 | tf_op jit(solution)/shard_map/pallas_call | solution.py:93
  145.2 11.4 %shard_map.78 = bf16[1024,768]{1,0:T(8,128)(2,1)S(1)} custom-call(bf16[1024,2048]{1,0:T(8,128)(2,1)} %get-tuple-element.12.ga_ref.g_ref, bf16[16,144,768]{2,1,0:T(8,128)(2,1)} %all_to_all.15.x_ref.xa_ref, bf16[1024,2048]{1,0:T(8,128)(2,1)} %get-tuple-element.13.gb_ref.g_ref, bf16[16,144,768]{2,1,0:T(8,128)(2,1)} %collective-permute-done.7.x_ref.xb_ref), custom_call_target="tpu_custom_call" | custom-call | flops 6442450944 | bytes 18874368 | tf_op jit(solution)/shard_map/pallas_call | solution.py:151
  156.6 1.2 copy-done.2
  157.8 6.7 %shard_map.80 = bf16[16,768,128]{2,1,0:T(8,128)(2,1)} custom-call(bf16[768,1024]{1,0:T(8,128)(2,1)S(1)} %bitcast.68, bf16[1024,2048]{1,0:T(8,128)(2,1)} %get-tuple-element.13.gb_ref.g_ref), custom_call_target="tpu_custom_call" | custom-call | flops 3221225472 | bytes 9437184 | tf_op jit(solution)/shard_map/pallas_call | solution.py:181
  164.5 3.1 %collective-permute-start.8 = (bf16[16,768,128]{2,1,0:T(8,128)(2,1)}, bf16[16,768,128]{2,1,0:T(8,128)(2,1)}, u32[]{:S(2)}, u32[]{:S(2)}) collective-permute-start(bf16[16,768,128]{2,1,0:T(8,128)(2,1)} %shard_map.80), channel_id=1, source_target_pairs={{0,1},{1,0},{2,3},{3,2},{4,5},{5,4},{6,7},{7,6},{8,9},{9,8},{10,11... | collective-permute-start | bytes 9437192 | tf_op jit(solution)/shard_map/ppermute | solution.py:297
  167.6 1.9 collective-permute-start.16
  169.5 4.1 %collective-permute-done.16 = bf16[16,128,128]{2,1,0:T(8,128)(2,1)S(1)} collective-permute-done((bf16[16,128,128]{2,1,0:T(8,128)(2,1)S(1)}, bf16[16,128,128]{2,1,0:T(8,128)(2,1)S(1)}, u32[]{:S(2)}, u32[]{:S(2)}) %collective-permute-start.16) | collective-permute-done | bytes 524320 | tf_op jit(solution)/shard_map/ppermute | solution.py:292
  173.6 1.1 pad_maximum_fusion.1
  174.7 4.3 %all-to-all-start.2 = ((bf16[16,256,128]{2,1,0:T(8,128)(2,1)}), bf16[16,256,128]{2,1,0:T(8,128)(2,1)}, u32[]{:S(2)}, u32[]{:S(2)}) async-start(bf16[16,256,128]{2,1,0:T(8,128)(2,1)} %pad_maximum_fusion.1), calls=%async_computation.2 | async-start | bytes 2097152 | tf_op jit(solution)/shard_map/all_to_all | solution.py:294
  179.0 5.5 %shard_map.79 = bf16[16,768,128]{2,1,0:T(8,128)(2,1)S(1)} custom-call(bf16[768,1024]{1,0:T(8,128)(2,1)S(1)} %bitcast.69, bf16[1024,2048]{1,0:T(8,128)(2,1)} %get-tuple-element.12.ga_ref.g_ref), custom_call_target="tpu_custom_call" | custom-call | flops 3221225472 | bytes 9437184 | tf_op jit(solution)/shard_map/pallas_call | solution.py:181
  184.5 4.3 %add_convert_fusion = bf16[16,768,128]{2,1,0:T(8,128)(2,1)} fusion(bf16[16,768,128]{2,1,0:T(8,128)(2,1)} %collective-permute-done.8, bf16[16,768,128]{2,1,0:T(8,128)(2,1)S(1)} %shard_map.79), kind=kLoop, calls=%fused_computation | loop fusion | flops 6291456 | bytes 9437184 | tf_op jit(solution)/shard_map/convert_element_type | solution.py:298
  188.9 7.2 %all-to-all-done.2.got_ref = bf16[16,256,128]{2,1,0:T(8,128)(2,1)} async-done(((bf16[16,256,128]{2,1,0:T(8,128)(2,1)}), bf16[16,256,128]{2,1,0:T(8,128)(2,1)}, u32[]{:S(2)}, u32[]{:S(2)}) %all-to-all-start.2) | async-done | bytes 1048608 | tf_op jit(solution)/shard_map/all_to_all | solution.py:294
  196.1 4.7 %all-to-all-start.1 = ((bf16[16,768,128]{2,1,0:T(8,128)(2,1)}), bf16[16,768,128]{2,1,0:T(8,128)(2,1)}, u32[]{:S(2)}, u32[]{:S(2)}) async-start(bf16[16,768,128]{2,1,0:T(8,128)(2,1)} %add_convert_fusion), calls=%async_computation.1 | async-start | bytes 6291456 | tf_op jit(solution)/shard_map/all_to_all | solution.py:299
  200.8 0.1 copy.59
  200.9 0.6 fusion
  201.5 0.1 slice_bitcast_fusion.1
  201.7 4.4 %collective-permute-start.10 = (bf16[4,64,768]{2,1,0:T(8,128)(2,1)S(1)}, bf16[4,64,768]{2,1,0:T(8,128)(2,1)S(1)}, u32[]{:S(2)}, u32[]{:S(2)}) collective-permute-start(bf16[4,64,768]{2,1,0:T(8,128)(2,1)S(1)} %pad_maximum_fusion.3), channel_id=1, source_target_pairs={{0,30},{2,0},{4,2},{6,4},{8,6},{10,8},{12,10},{14,12},{16,14},{18,... | collective-permute-start | bytes 1179656 | tf_op jit(solution)/shard_map/ppermute | solution.py:198
  206.1 3.0 %collective-permute-start.12 = (bf16[4,32,768]{2,1,0:T(8,128)(2,1)S(1)}, bf16[4,32,768]{2,1,0:T(8,128)(2,1)S(1)}, u32[]{:S(2)}, u32[]{:S(2)}) collective-permute-start(bf16[4,32,768]{2,1,0:T(8,128)(2,1)S(1)} %pad_maximum_fusion.5), channel_id=1, source_target_pairs={{0,28},{2,30},{4,0},{6,2},{8,4},{10,6},{12,8},{14,10},{16,12},{18,... | collective-permute-start | bytes 589832 | tf_op jit(solution)/shard_map/ppermute | solution.py:198
  209.2 3.2 %collective-permute-start.11 = (bf16[4,32,768]{2,1,0:T(8,128)(2,1)S(1)}, bf16[4,32,768]{2,1,0:T(8,128)(2,1)S(1)}, u32[]{:S(2)}, u32[]{:S(2)}) collective-permute-start(bf16[4,32,768]{2,1,0:T(8,128)(2,1)S(1)} %slice.110), channel_id=1, source_target_pairs={{0,4},{2,6},{4,8},{6,10},{8,12},{10,14},{12,16},{14,18},{16,20},{1... | collective-permute-start | bytes 589832 | tf_op jit(solution)/shard_map/ppermute | solution.py:198
  212.3 1.9 collective-permute-start.9
  214.3 0.2 fusion.26
  214.4 0.7 select_reduce_fusion
  215.2 5.7 %collective-permute-done.12 = bf16[4,32,768]{2,1,0:T(8,128)(2,1)S(1)} collective-permute-done((bf16[4,32,768]{2,1,0:T(8,128)(2,1)S(1)}, bf16[4,32,768]{2,1,0:T(8,128)(2,1)S(1)}, u32[]{:S(2)}, u32[]{:S(2)}) %collective-permute-start.12) | collective-permute-done | bytes 196640 | tf_op jit(solution)/shard_map/ppermute | solution.py:198
  220.9 9.1 %collective-permute-done.9 = bf16[4,64,768]{2,1,0:T(8,128)(2,1)S(1)} collective-permute-done((bf16[4,64,768]{2,1,0:T(8,128)(2,1)S(1)}, bf16[4,64,768]{2,1,0:T(8,128)(2,1)S(1)}, u32[]{:S(2)}, u32[]{:S(2)}) %collective-permute-start.9) | collective-permute-done | bytes 393248 | tf_op jit(solution)/shard_map/ppermute | solution.py:198
  230.0 1.1 fusion.33
  231.1 3.5 %collective-permute-start.13 = (bf16[64,768]{1,0:T(8,128)(2,1)S(1)}, bf16[64,768]{1,0:T(8,128)(2,1)S(1)}, u32[]{:S(2)}, u32[]{:S(2)}) collective-permute-start(bf16[64,768]{1,0:T(8,128)(2,1)S(1)} %get-tuple-element.30), channel_id=1, source_target_pairs={{0,8},{2,10},{4,12},{6,14},{8,16},{10,18},{12,20},{14,22},{16,24},... | collective-permute-start | bytes 294920 | tf_op jit(solution)/shard_map/ppermute | solution.py:198
  234.7 8.8 %collective-permute-start.14 = (bf16[64,768]{1,0:T(8,128)(2,1)S(1)}, bf16[64,768]{1,0:T(8,128)(2,1)S(1)}, u32[]{:S(2)}, u32[]{:S(2)}) collective-permute-start(bf16[64,768]{1,0:T(8,128)(2,1)S(1)} %get-tuple-element.32), channel_id=1, source_target_pairs={{0,16},{2,18},{4,20},{6,22},{8,24},{10,26},{12,28},{14,30},{16,0},... | collective-permute-start | bytes 294920 | tf_op jit(solution)/shard_map/ppermute | solution.py:198
  243.5 4.0 %collective-permute-start.15 = (bf16[64,768]{1,0:T(8,128)(2,1)S(1)}, bf16[64,768]{1,0:T(8,128)(2,1)S(1)}, u32[]{:S(2)}, u32[]{:S(2)}) collective-permute-start(bf16[64,768]{1,0:T(8,128)(2,1)S(1)} %get-tuple-element.31), channel_id=1, source_target_pairs={{0,24},{2,26},{4,28},{6,30},{8,0},{10,2},{12,4},{14,6},{16,8},{18,... | collective-permute-start | bytes 294920 | tf_op jit(solution)/shard_map/ppermute | solution.py:198
  247.5 0.2 fusion.12
  247.7 0.1 broadcast_in_dim.42
  247.8 1.2 collective-permute-done.13
  249.0 8.4 %collective-permute-done.14 = bf16[64,768]{1,0:T(8,128)(2,1)S(1)} collective-permute-done((bf16[64,768]{1,0:T(8,128)(2,1)S(1)}, bf16[64,768]{1,0:T(8,128)(2,1)S(1)}, u32[]{:S(2)}, u32[]{:S(2)}) %collective-permute-start.14) | collective-permute-done | bytes 98336 | tf_op jit(solution)/shard_map/ppermute | solution.py:198
  257.4 6.4 %collective-permute-done.15 = bf16[64,768]{1,0:T(8,128)(2,1)S(1)} collective-permute-done((bf16[64,768]{1,0:T(8,128)(2,1)S(1)}, bf16[64,768]{1,0:T(8,128)(2,1)S(1)}, u32[]{:S(2)}, u32[]{:S(2)}) %collective-permute-start.15) | collective-permute-done | bytes 98336 | tf_op jit(solution)/shard_map/ppermute | solution.py:198
  263.8 1.6 fusion.5
  265.5 0.3 broadcast_in_dim.43.key_ref
  265.8 6.9 %shard_map.81 = bf16[2048,128]{1,0:T(8,128)(2,1)} custom-call(s32[2048,256]{1,0:T(8,128)S(1)} %broadcast_in_dim.43.key_ref, bf16[16,256,128]{2,1,0:T(8,128)(2,1)} %all-to-all-done.2.got_ref), custom_call_target="tpu_custom_call" | custom-call | flops 2147483648 | bytes 8388608 | tf_op jit(solution)/shard_map/pallas_call | solution.py:255
  272.7 2.4 reduce_sum.21
  275.1 0.8 copy.64
  (33 shorter events, 0.3 us)
Async XLA Ops:
  0.6 58.1 %copy-start = (bf16[1024,768]{1,0:T(8,128)(2,1)S(1)}, bf16[1024,768]{1,0:T(8,128)(2,1)}, u32[]{:S(2)}) copy-start(bf16[1024,768]{1,0:T(8,128)(2,1)} %param.6) | copy-start | bytes 4718596
  52.9 83.5 %collective-permute-start.7 = (bf16[16,144,768]{2,1,0:T(8,128)(2,1)}, bf16[16,144,768]{2,1,0:T(8,128)(2,1)}, u32[]{:S(2)}, u32[]{:S(2)}) collective-permute-start(bf16[16,144,768]{2,1,0:T(8,128)(2,1)} %all_to_all.15.x_ref.xa_ref), channel_id=1, source_target_pairs={{0,1},{1,0},{2,3},{3,2},{4,5},{5,4},{6,7},{7,6},{8,9},{9,8},{10,11... | collective-permute-start | bytes 10616840 | tf_op jit(solution)/shard_map/ppermute | solution.py:288
  58.8 26.4 %collective-permute-start = (bf16[64,768]{1,0:T(8,128)(2,1)S(1)}, bf16[64,768]{1,0:T(8,128)(2,1)S(1)}, u32[]{:S(2)}, u32[]{:S(2)}) collective-permute-start(bf16[64,768]{1,0:T(8,128)(2,1)S(1)} %constant_dynamic-slice_fusion), channel_id=1, source_target_pairs={{0,24},{2,26},{4,28},{6,30},{8,0},{10,2},{12,4},{14,6},{16,8},{18,... | collective-permute-start | bytes 294920 | tf_op jit(solution)/shard_map/ppermute | solution.py:198
  71.0 14.9 %collective-permute-start.1 = (bf16[64,768]{1,0:T(8,128)(2,1)S(1)}, bf16[64,768]{1,0:T(8,128)(2,1)S(1)}, u32[]{:S(2)}, u32[]{:S(2)}) collective-permute-start(bf16[64,768]{1,0:T(8,128)(2,1)S(1)} %constant_dynamic-slice_fusion), channel_id=1, source_target_pairs={{0,16},{2,18},{4,20},{6,22},{8,24},{10,26},{12,28},{14,30},{16,0},... | collective-permute-start | bytes 294920 | tf_op jit(solution)/shard_map/ppermute | solution.py:198
  75.9 13.7 %collective-permute-start.2 = (bf16[64,768]{1,0:T(8,128)(2,1)S(1)}, bf16[64,768]{1,0:T(8,128)(2,1)S(1)}, u32[]{:S(2)}, u32[]{:S(2)}) collective-permute-start(bf16[64,768]{1,0:T(8,128)(2,1)S(1)} %constant_dynamic-slice_fusion), channel_id=1, source_target_pairs={{0,8},{2,10},{4,12},{6,14},{8,16},{10,18},{12,20},{14,22},{16,24},... | collective-permute-start | bytes 294920 | tf_op jit(solution)/shard_map/ppermute | solution.py:198
  89.7 32.1 %collective-permute-start.6 = (bf16[4,64,768]{2,1,0:T(8,128)(2,1)S(1)}, bf16[4,64,768]{2,1,0:T(8,128)(2,1)S(1)}, u32[]{:S(2)}, u32[]{:S(2)}) collective-permute-start(bf16[4,64,768]{2,1,0:T(8,128)(2,1)S(1)} %get-tuple-element.34), channel_id=1, source_target_pairs={{0,2},{2,4},{4,6},{6,8},{8,10},{10,12},{12,14},{14,16},{16,18},{18... | collective-permute-start | bytes 1179656 | tf_op jit(solution)/shard_map/ppermute | solution.py:198
  96.1 24.7 %collective-permute-start.5 = (bf16[4,32,768]{2,1,0:T(8,128)(2,1)S(1)}, bf16[4,32,768]{2,1,0:T(8,128)(2,1)S(1)}, u32[]{:S(2)}, u32[]{:S(2)}) collective-permute-start(bf16[4,32,768]{2,1,0:T(8,128)(2,1)S(1)} %get-tuple-element.36), channel_id=1, source_target_pairs={{0,4},{2,6},{4,8},{6,10},{8,12},{10,14},{12,16},{14,18},{16,20},{1... | collective-permute-start | bytes 589832 | tf_op jit(solution)/shard_map/ppermute | solution.py:198
  103.1 17.7 %collective-permute-start.4 = (bf16[4,32,768]{2,1,0:T(8,128)(2,1)S(1)}, bf16[4,32,768]{2,1,0:T(8,128)(2,1)}, u32[]{:S(2)}, u32[]{:S(2)}) collective-permute-start(bf16[4,32,768]{2,1,0:T(8,128)(2,1)S(1)} %get-tuple-element.35), channel_id=1, source_target_pairs={{0,28},{2,30},{4,0},{6,2},{8,4},{10,6},{12,8},{14,10},{16,12},{18,... | collective-permute-start | bytes 589832 | tf_op jit(solution)/shard_map/ppermute | solution.py:198
  107.5 17.4 %collective-permute-start.3 = (bf16[4,64,768]{2,1,0:T(8,128)(2,1)S(1)}, bf16[4,64,768]{2,1,0:T(8,128)(2,1)}, u32[]{:S(2)}, u32[]{:S(2)}) collective-permute-start(bf16[4,64,768]{2,1,0:T(8,128)(2,1)S(1)} %get-tuple-element.34), channel_id=1, source_target_pairs={{0,30},{2,0},{4,2},{6,4},{8,6},{10,8},{12,10},{14,12},{16,14},{18,... | collective-permute-start | bytes 1179656 | tf_op jit(solution)/shard_map/ppermute | solution.py:198
  145.2 12.6 %copy-start.1 = (bf16[1024,768]{0,1:T(8,128)(2,1)S(1)}, bf16[1024,768]{0,1:T(8,128)(2,1)}, u32[]{:S(2)}) copy-start(bf16[1024,768]{0,1:T(8,128)(2,1)} %copy.53) | copy-start | bytes 4718596
  156.6 1.2 copy-start.2
  164.5 20.1 %collective-permute-start.8 = (bf16[16,768,128]{2,1,0:T(8,128)(2,1)}, bf16[16,768,128]{2,1,0:T(8,128)(2,1)}, u32[]{:S(2)}, u32[]{:S(2)}) collective-permute-start(bf16[16,768,128]{2,1,0:T(8,128)(2,1)} %shard_map.80), channel_id=1, source_target_pairs={{0,1},{1,0},{2,3},{3,2},{4,5},{5,4},{6,7},{7,6},{8,9},{9,8},{10,11... | collective-permute-start | bytes 9437192 | tf_op jit(solution)/shard_map/ppermute | solution.py:297
  167.6 6.0 %collective-permute-start.16 = (bf16[16,128,128]{2,1,0:T(8,128)(2,1)S(1)}, bf16[16,128,128]{2,1,0:T(8,128)(2,1)S(1)}, u32[]{:S(2)}, u32[]{:S(2)}) collective-permute-start(bf16[16,128,128]{2,1,0:T(8,128)(2,1)S(1)} %get-tuple-element.16), channel_id=1, source_target_pairs={{0,1},{1,0},{2,3},{3,2},{4,5},{5,4},{6,7},{7,6},{8,9},{9,8},{10,11... | collective-permute-start | bytes 1572872 | tf_op jit(solution)/shard_map/ppermute | solution.py:292
  174.7 21.4 %all-to-all-start.2 = ((bf16[16,256,128]{2,1,0:T(8,128)(2,1)}), bf16[16,256,128]{2,1,0:T(8,128)(2,1)}, u32[]{:S(2)}, u32[]{:S(2)}) async-start(bf16[16,256,128]{2,1,0:T(8,128)(2,1)} %pad_maximum_fusion.1), calls=%async_computation.2 | async-start | bytes 2097152 | tf_op jit(solution)/shard_map/all_to_all | solution.py:294
  188.9 11.9 %copy-start.4 = (s32[128,16]{0,1:T(8,128)S(1)}, s32[128,16]{0,1:T(8,128)}, u32[]{:S(2)}) copy-start(s32[128,16]{0,1:T(8,128)} %param.7) | copy-start | bytes 24580
  188.9 12.6 %copy-start.3 = (bf16[1024,768]{1,0:T(8,128)(2,1)S(1)}, bf16[1024,768]{1,0:T(8,128)(2,1)}, u32[]{:S(2)}) copy-start(bf16[1024,768]{1,0:T(8,128)(2,1)} %copy-done.2) | copy-start | bytes 4718596
  196.1 76.6 %all-to-all-start.1 = ((bf16[16,768,128]{2,1,0:T(8,128)(2,1)}), bf16[16,768,128]{2,1,0:T(8,128)(2,1)}, u32[]{:S(2)}, u32[]{:S(2)}) async-start(bf16[16,768,128]{2,1,0:T(8,128)(2,1)} %add_convert_fusion), calls=%async_computation.1 | async-start | bytes 6291456 | tf_op jit(solution)/shard_map/all_to_all | solution.py:299
  201.7 19.2 %collective-permute-start.10 = (bf16[4,64,768]{2,1,0:T(8,128)(2,1)S(1)}, bf16[4,64,768]{2,1,0:T(8,128)(2,1)S(1)}, u32[]{:S(2)}, u32[]{:S(2)}) collective-permute-start(bf16[4,64,768]{2,1,0:T(8,128)(2,1)S(1)} %pad_maximum_fusion.3), channel_id=1, source_target_pairs={{0,30},{2,0},{4,2},{6,4},{8,6},{10,8},{12,10},{14,12},{16,14},{18,... | collective-permute-start | bytes 1179656 | tf_op jit(solution)/shard_map/ppermute | solution.py:198
  206.1 14.7 %collective-permute-start.12 = (bf16[4,32,768]{2,1,0:T(8,128)(2,1)S(1)}, bf16[4,32,768]{2,1,0:T(8,128)(2,1)S(1)}, u32[]{:S(2)}, u32[]{:S(2)}) collective-permute-start(bf16[4,32,768]{2,1,0:T(8,128)(2,1)S(1)} %pad_maximum_fusion.5), channel_id=1, source_target_pairs={{0,28},{2,30},{4,0},{6,2},{8,4},{10,6},{12,8},{14,10},{16,12},{18,... | collective-permute-start | bytes 589832 | tf_op jit(solution)/shard_map/ppermute | solution.py:198
  209.2 11.7 %collective-permute-start.11 = (bf16[4,32,768]{2,1,0:T(8,128)(2,1)S(1)}, bf16[4,32,768]{2,1,0:T(8,128)(2,1)S(1)}, u32[]{:S(2)}, u32[]{:S(2)}) collective-permute-start(bf16[4,32,768]{2,1,0:T(8,128)(2,1)S(1)} %slice.110), channel_id=1, source_target_pairs={{0,4},{2,6},{4,8},{6,10},{8,12},{10,14},{12,16},{14,18},{16,20},{1... | collective-permute-start | bytes 589832 | tf_op jit(solution)/shard_map/ppermute | solution.py:198
  212.3 17.7 %collective-permute-start.9 = (bf16[4,64,768]{2,1,0:T(8,128)(2,1)S(1)}, bf16[4,64,768]{2,1,0:T(8,128)(2,1)S(1)}, u32[]{:S(2)}, u32[]{:S(2)}) collective-permute-start(bf16[4,64,768]{2,1,0:T(8,128)(2,1)S(1)} %get-tuple-element.28), channel_id=1, source_target_pairs={{0,2},{2,4},{4,6},{6,8},{8,10},{10,12},{12,14},{14,16},{16,18},{18... | collective-permute-start | bytes 1179656 | tf_op jit(solution)/shard_map/ppermute | solution.py:198
  231.1 17.9 %collective-permute-start.13 = (bf16[64,768]{1,0:T(8,128)(2,1)S(1)}, bf16[64,768]{1,0:T(8,128)(2,1)S(1)}, u32[]{:S(2)}, u32[]{:S(2)}) collective-permute-start(bf16[64,768]{1,0:T(8,128)(2,1)S(1)} %get-tuple-element.30), channel_id=1, source_target_pairs={{0,8},{2,10},{4,12},{6,14},{8,16},{10,18},{12,20},{14,22},{16,24},... | collective-permute-start | bytes 294920 | tf_op jit(solution)/shard_map/ppermute | solution.py:198
  234.7 22.7 %collective-permute-start.14 = (bf16[64,768]{1,0:T(8,128)(2,1)S(1)}, bf16[64,768]{1,0:T(8,128)(2,1)S(1)}, u32[]{:S(2)}, u32[]{:S(2)}) collective-permute-start(bf16[64,768]{1,0:T(8,128)(2,1)S(1)} %get-tuple-element.32), channel_id=1, source_target_pairs={{0,16},{2,18},{4,20},{6,22},{8,24},{10,26},{12,28},{14,30},{16,0},... | collective-permute-start | bytes 294920 | tf_op jit(solution)/shard_map/ppermute | solution.py:198
  243.5 20.3 %collective-permute-start.15 = (bf16[64,768]{1,0:T(8,128)(2,1)S(1)}, bf16[64,768]{1,0:T(8,128)(2,1)S(1)}, u32[]{:S(2)}, u32[]{:S(2)}) collective-permute-start(bf16[64,768]{1,0:T(8,128)(2,1)S(1)} %get-tuple-element.31), channel_id=1, source_target_pairs={{0,24},{2,26},{4,28},{6,30},{8,0},{10,2},{12,4},{14,6},{16,8},{18,... | collective-permute-start | bytes 294920 | tf_op jit(solution)/shard_map/ppermute | solution.py:198

commit v3 on v2

--- a/solution.py
+++ b/solution.py
@@ -30,8 +30,7 @@
     offset = (meta[1] * HALF + 2).astype(F32)
     n = STEP * ROWS
     x = x_ref[:, :ROWS, :].reshape(n, D)
-    chunk = lax.rem(lax.broadcasted_iota(jnp.int32, (Z, ROWS), 0) + meta[2], Z)
-    wanted = chunk.astype(F32) * 16.0 + base
+    wanted = lax.broadcasted_iota(jnp.int32, (Z, ROWS), 0).astype(F32) * 16.0 + base
     before = (
         lax.broadcasted_iota(jnp.int32, (ROWS, ROWS), 0)
         < lax.broadcasted_iota(jnp.int32, (ROWS, ROWS), 1)
@@ -50,6 +49,7 @@
         entries.append(entry)
         ranks.append(jnp.where(named, rank, -1.0))
     entry = jnp.concatenate(entries, axis=1)
+    gain = jnp.where(entry >= 2.0, 0.5, 0.0)
     place = lax.broadcasted_iota(jnp.int32, (HALF, n), 0).astype(F32) + offset
     part = 4 * HALF
     for q in range(COLS // part):
@@ -60,8 +60,8 @@
             z = 4 * q + s
             code = jnp.broadcast_to(entry[z : z + 1, :], (HALF, n))
             own = logits[s * HALF : (s + 1) * HALF, :]
-            sig = 0.5 * jnp.tanh(0.5 * own) + 0.5
-            value = jnp.where(code >= 2.0, jnp.where(code == place, sig - 1.0, sig), 0.0)
+            sig = (jnp.tanh(0.5 * own) + 1.0) * jnp.broadcast_to(gain[z : z + 1, :], (HALF, n))
+            value = jnp.where(code == place, sig - 1.0, sig)
             grad[z * HALF : (z + 1) * HALF, :] = value.astype(BF16)
     slot = lax.broadcasted_iota(jnp.int32, (MOST, ROWS), 0).astype(F32)
     lane = lax.broadcasted_iota(jnp.int32, (HALF, ROWS), 1) // MOST
@@ -194,35 +194,6 @@
     )(wt, g)
 
 
-def shift(x, k):
-    return lax.ppermute(x, "z", [(s, (s - k) % Z) for s in range(Z)])
-
-
-def gather_z(mine):
-    ahead, behind, across = shift(mine, 4), shift(mine, -4), shift(mine, 8)
-    every = jnp.stack([mine, ahead, across, behind])
-    half = HALF // 2
-    one, last = shift(every, 1), shift(every, -1)
-    low, high = shift(every[:, :half], 2), shift(every[:, half:], -2)
-    two = jnp.concatenate([low, jnp.roll(high, -1, axis=0)], axis=1)
-    parts = [every, one, two, jnp.roll(last, -1, axis=0)]
-    return jnp.stack(parts, axis=1).reshape((Z,) + mine.shape)
-
-
-def reduce_z(total):
-    half = HALF // 2
-    total = total.reshape(4, 4, HALF, D)
-    last = jnp.roll(total[:, 3], 1, axis=0)
-    two = total[:, 2]
-    one, last = shift(total[:, 1], -1), shift(last, 1)
-    low, high = shift(two[:, :half], -2), shift(jnp.roll(two[:, half:], 1, axis=0), 2)
-    every = total[:, 0].astype(F32) + one.astype(F32) + last.astype(F32)
-    every = every + jnp.concatenate([low, high], axis=1).astype(F32)
-    sent = every[1:].astype(BF16)
-    got = [shift(sent[0], -4), shift(sent[1], 8), shift(sent[2], 4)]
-    return every[0] + got[0].astype(F32) + got[1].astype(F32) + got[2].astype(F32)
-
-
 def unpack_body(key_ref, got_ref, out_ref):
     key = key_ref[...]
     lane = lax.broadcasted_iota(jnp.int32, (1, 2 * ROWS), 1)
@@ -271,11 +242,9 @@
 def shards(features, weights, block_ids, label_codes, counts):
     inst = lax.axis_index(PLANE)
     core = lax.axis_index("core")
-    depth = lax.axis_index("z")
-    meta = jnp.stack([8 * core + inst // 2, inst % 2, depth]).astype(jnp.int32)
+    meta = jnp.stack([8 * core + inst // 2, inst % 2]).astype(jnp.int32)
     mine = lax.dynamic_slice_in_dim(weights, inst * HALF, HALF, 0)
-    w = gather_z(mine).reshape(COLS, D)
-    wt = w.T
+    w = lax.all_gather(mine, "z").reshape(COLS, D)
 
     alive = jnp.arange(TOP, dtype=jnp.int32)[None, :] < counts[:, None]
     code = jnp.where(alive, jnp.minimum(label_codes, BS) + 2, 1)
@@ -285,16 +254,22 @@
     copies = jnp.broadcast_to(sent[None], (Z,) + sent.shape)
     own = lax.all_to_all(copies, PLANE, split_axis=0, concat_axis=0, tiled=True)
     swap = [(0, 1), (1, 0)]
+    own, w = lax.optimization_barrier((own, w))
+    wt = w.T
     other = lax.ppermute(own, "core", swap)
     own_grad, own_pack = expert(meta, own, w)
     other_grad, other_pack = expert(meta, other, w)
+    other_rows = row_grad(wt, other_grad)
+    other_rows, own_grad = lax.optimization_barrier((other_rows, own_grad))
+    back_rows = lax.ppermute(other_rows, "core", swap)
+    back_pack = lax.ppermute(other_pack, "core", swap)
     total = weight_grad(own_grad, own, other_grad, other)
-    back_pack = lax.ppermute(other_pack, "core", swap)
+    total, own_grad = lax.optimization_barrier((total, own_grad))
+    grad_w = lax.psum_scatter(
+        total.reshape(Z, HALF, D), "z", scatter_dimension=0, tiled=False
+    ).astype(F32)
     packs = jnp.concatenate([own_pack, back_pack], axis=1)
     got = lax.all_to_all(packs, PLANE, split_axis=0, concat_axis=0, tiled=True)
-    total, other_grad, own_grad = lax.optimization_barrier((total, other_grad, own_grad))
-    grad_w = reduce_z(total)
-    back_rows = lax.ppermute(row_grad(wt, other_grad), "core", swap)
     sums = (row_grad(wt, own_grad).astype(F32) + back_rows.astype(F32)).astype(BF16)
     got_rows = lax.all_to_all(sums, PLANE, split_axis=0, concat_axis=0, tiled=True)
     grad_x = jnp.sum(got_rows, axis=0, dtype=F32).T.astype(BF16)
@@ -306,7 +281,7 @@
     rank = jnp.dot(before, named, preferred_element_type=F32)
     rank = jnp.sum(jnp.where(block_ids[:, :, None] == blocks, rank[:, None, :], 0.0), axis=2)
     rank = rank.astype(jnp.int32)
-    row = (block_ids // 16 - depth) % Z
+    row = block_ids // 16
     owner = block_ids % 16
     crossed = (owner // 8) ^ core
     key = (((owner % 8) * 2 + crossed) * 2 + row // 8) * ROWS + (row % 8) * MOST + rank

time: 277 us -> 239 us (0.86)
  the two profiles are of different devices: /device:TPU:1 before, /device:TPU:2 now
where the time goes in v3:
time: 239 us; the launch traced here: 238 us
  waiting for transfers between devices  123 us (51%)
  Pallas kernels  47.5 us (20%)
  starting transfers between devices  31.2 us (13%)
  between operations  14.2 us (6%)
  other arithmetic  13.6 us (6%)
  local copies, waits for them, and re-layouts  8.61 us (4%)
    all_gather x1, waiting for transfers between devices, shards(): w = lax.all_gather(mine, 'z').reshape(COLS, D)  76.4 us
    reduce_scatter x1, waiting for transfers between devices, shards(): lax.psum_scatter(total.reshape(Z, HALF, D), 'z', scatter_dimension=0, til...  42.3 us
    pallas_call x2, Pallas kernels, expert(): pl.pallas_call(expert_body, grid_spec=pltpu.PrefetchScalarGridSpec(num_sc...  17.1 us
    pallas_call x2, Pallas kernels, row_grad(): pl.pallas_call(row_body, grid=(count // STEP,), in_specs=[pl.BlockSpec((D...  12.1 us
    pallas_call x1, Pallas kernels, weight_grad(): pl.pallas_call(weight_body, grid=(2 * half,), in_specs=[pl.BlockSpec((COL...  11.4 us
    all_to_all x1, starting transfers between devices, shards(): own = lax.all_to_all(copies, PLANE, split_axis=0, concat_axis=0, tiled=True)  10.2 us
    all_to_all x1, starting transfers between devices, shards(): lax.all_to_all(sums, PLANE, split_axis=0, concat_axis=0, tiled=True)  7.36 us
    all_to_all x1, starting transfers between devices, shards(): got = lax.all_to_all(packs, PLANE, split_axis=0, concat_axis=0, tiled=True)  7.26 us
  transfers between devices with their start and end apart: 8, of which 3 were waited for; matrix products, arithmetic and copies ran while one was open for 5% of the time, Pallas kernels for 14%

profile of v3, /device:TPU:2, one launch (start us, length us, event | category | flops | bytes accessed | tf_op | source)
XLA Modules:
  0.0 238.1 jit_solution(3937441699998472538)
XLA Ops:
  7.2 0.0 copy-start
  7.2 0.8 convert_bitcast_fusion
  8.0 0.8 copy.31
  8.8 0.7 fusion.23
  9.5 0.1 copy.32
  9.6 1.0 pad_maximum_fusion.1
  10.6 2.0 broadcast_in_dim.23
  12.6 10.2 %all-to-all-start = ((bf16[16,144,768]{2,1,0:T(8,128)(2,1)}), bf16[16,144,768]{2,1,0:T(8,128)(2,1)}, u32[]{:S(2)}, u32[]{:S(2)}) async-start(bf16[16,144,768]{2,1,0:T(8,128)(2,1)} %broadcast_in_dim.23), calls=%async_computation | async-start | bytes 7077888 | tf_op jit(solution)/shard_map/all_to_all | solution.py:255
  22.7 0.0 all-gather.3.cloned.1.call-start
  22.8 0.0 copy-done
  22.8 0.7 constant_dynamic-slice_fusion
  23.4 0.0 all-gather.3.cloned.1.call-update
  23.4 76.4 %all-gather.3.cloned.1.call-done.w_ref = bf16[1024,768]{1,0:T(8,128)(2,1)} async-done(((bf16[64,768]{1,0:T(8,128)(2,1)}), bf16[1024,768]{1,0:T(8,128)(2,1)}) %all-gather.3.cloned.1.call-update) | async-done | bytes 1572880 | tf_op jit(solution)/shard_map/all_gather | solution.py:247
  99.8 0.0 copy-start.1
  99.8 0.0 all-to-all-done.x_ref.xa_ref
  99.8 2.0 collective-permute-start
  101.9 0.1 pad_add_fusion.meta
  102.0 2.6 %copy.33 = bf16[1024,768]{0,1:T(8,128)(2,1)} copy(bf16[1024,768]{1,0:T(8,128)(2,1)} %all-gather.3.cloned.1.call-done.w_ref) | data formatting | bytes 3145728 | tf_op jit(solution)/shard_map/optimization_barrier | solution.py:257
  104.6 0.0 copy-done.1
  104.6 8.5 %shard_map.78 = (bf16[1024,2048]{1,0:T(8,128)(2,1)}, bf16[16,128,128]{2,1,0:T(8,128)(2,1)S(1)}) custom-call(s32[2]{0:T(128)S(1)} %pad_add_fusion.meta, bf16[16,144,768]{2,1,0:T(8,128)(2,1)} %all-to-all-done.x_ref.xa_ref, bf16[1024,768]{1,0:T(8,128)(2,1)S(1)} %copy-done.1), custom_call_target="tpu_custom_call" | custom-call | flops 3221225472 | bytes 10485760 | tf_op jit(solution)/shard_map/pallas_call | solution.py:93
  113.1 0.0 copy-start.2
  113.1 0.0 collective-permute-done.x_ref.xb_ref
  113.1 8.5 %shard_map.76 = (bf16[1024,2048]{1,0:T(8,128)(2,1)}, bf16[16,128,128]{2,1,0:T(8,128)(2,1)S(1)}) custom-call(s32[2]{0:T(128)S(1)} %pad_add_fusion.meta, bf16[16,144,768]{2,1,0:T(8,128)(2,1)} %collective-permute-done.x_ref.xb_ref, bf16[1024,768]{1,0:T(8,128)(2,1)S(1)} %copy-done.1), custom_call_target="tpu_custom_call" | custom-call | flops 3221225472 | bytes 10485760 | tf_op jit(solution)/shard_map/pallas_call | solution.py:93
  121.7 0.0 copy-done.2
  121.7 6.7 %shard_map.77 = bf16[16,768,128]{2,1,0:T(8,128)(2,1)} custom-call(bf16[768,1024]{1,0:T(8,128)(2,1)S(1)} %bitcast.14, bf16[1024,2048]{1,0:T(8,128)(2,1)} %get-tuple-element.15.g_ref.gb_ref), custom_call_target="tpu_custom_call" | custom-call | flops 3221225472 | bytes 9437184 | tf_op jit(solution)/shard_map/pallas_call | solution.py:181
  128.3 2.4 %collective-permute-start.1 = (bf16[16,768,128]{2,1,0:T(8,128)(2,1)}, bf16[16,768,128]{2,1,0:T(8,128)(2,1)}, u32[]{:S(2)}, u32[]{:S(2)}) collective-permute-start(bf16[16,768,128]{2,1,0:T(8,128)(2,1)} %shard_map.77), channel_id=1, source_target_pairs={{0,1},{1,0},{2,3},{3,2},{4,5},{5,4},{6,7},{7,6},{8,9},{9,8},{10,11... | collective-permute-start | bytes 9437192 | tf_op jit(solution)/shard_map/ppermute | solution.py:264
  130.7 1.9 collective-permute-start.2
  132.7 4.1 %collective-permute-done.2 = bf16[16,128,128]{2,1,0:T(8,128)(2,1)S(1)} collective-permute-done((bf16[16,128,128]{2,1,0:T(8,128)(2,1)S(1)}, bf16[16,128,128]{2,1,0:T(8,128)(2,1)S(1)}, u32[]{:S(2)}, u32[]{:S(2)}) %collective-permute-start.2) | collective-permute-done | bytes 524320 | tf_op jit(solution)/shard_map/ppermute | solution.py:265
  136.7 1.2 pad_maximum_fusion
  137.9 7.3 %all-to-all-start.2 = ((bf16[16,256,128]{2,1,0:T(8,128)(2,1)}), bf16[16,256,128]{2,1,0:T(8,128)(2,1)}, u32[]{:S(2)}, u32[]{:S(2)}) async-start(bf16[16,256,128]{2,1,0:T(8,128)(2,1)} %pad_maximum_fusion), calls=%async_computation.3 | async-start | bytes 2097152 | tf_op jit(solution)/shard_map/all_to_all | solution.py:272
  145.2 0.0 copy-start.3
  145.2 0.0 reduce-scatter.2.cloned.1.call-start
  145.2 11.4 %shard_map.79 = bf16[1024,768]{1,0:T(8,128)(2,1)S(1)} custom-call(bf16[1024,2048]{1,0:T(8,128)(2,1)} %get-tuple-element.18.ga_ref.g_ref, bf16[16,144,768]{2,1,0:T(8,128)(2,1)} %all-to-all-done.x_ref.xa_ref, bf16[1024,2048]{1,0:T(8,128)(2,1)} %get-tuple-element.15.g_ref.gb_ref, bf16[16,144,768]{2,1,0:T(8,128)(2,1)} %collective-permute-done.x_ref.xb_ref), custom_call_target="tpu_custom_call" | custom-call | flops 6442450944 | bytes 18874368 | tf_op jit(solution)/shard_map/pallas_call | solution.py:151
  156.6 0.0 copy-start.4
  156.6 1.2 copy-done.4
  157.8 0.0 reduce-scatter.2.cloned.1.call-update
  157.8 0.0 copy-done.3
  157.8 5.5 %shard_map.80 = bf16[16,768,128]{2,1,0:T(8,128)(2,1)S(1)} custom-call(bf16[768,1024]{1,0:T(8,128)(2,1)S(1)} %bitcast.15, bf16[1024,2048]{1,0:T(8,128)(2,1)} %get-tuple-element.18.ga_ref.g_ref), custom_call_target="tpu_custom_call" | custom-call | flops 3221225472 | bytes 9437184 | tf_op jit(solution)/shard_map/pallas_call | solution.py:181
  163.3 0.0 collective-permute-done.1
  163.3 4.3 %add_convert_fusion = bf16[16,768,128]{2,1,0:T(8,128)(2,1)} fusion(bf16[16,768,128]{2,1,0:T(8,128)(2,1)} %collective-permute-done.1, bf16[16,768,128]{2,1,0:T(8,128)(2,1)S(1)} %shard_map.80), kind=kLoop, calls=%fused_computation | loop fusion | flops 6291456 | bytes 9437184 | tf_op jit(solution)/shard_map/convert_element_type | solution.py:273
  167.6 0.0 copy-start.5
  167.6 0.0 all-to-all-done.2.got_ref
  167.7 7.4 %all-to-all-start.1 = ((bf16[16,768,128]{2,1,0:T(8,128)(2,1)}), bf16[16,768,128]{2,1,0:T(8,128)(2,1)}, u32[]{:S(2)}, u32[]{:S(2)}) async-start(bf16[16,768,128]{2,1,0:T(8,128)(2,1)} %add_convert_fusion), calls=%async_computation.1 | async-start | bytes 6291456 | tf_op jit(solution)/shard_map/all_to_all | solution.py:274
  175.0 0.0 copy-done.5
  175.0 0.1 copy.34
  175.1 0.6 fusion
  175.7 0.2 fusion.19
  175.9 0.7 select_reduce_fusion
  176.6 0.2 fusion.7
  176.8 0.1 broadcast_in_dim.42
  176.9 0.3 broadcast_in_dim.43.key_ref
  177.2 6.9 %shard_map.81 = bf16[2048,128]{1,0:T(8,128)(2,1)} custom-call(s32[2048,256]{1,0:T(8,128)S(1)} %broadcast_in_dim.43.key_ref, bf16[16,256,128]{2,1,0:T(8,128)(2,1)} %all-to-all-done.2.got_ref), custom_call_target="tpu_custom_call" | custom-call | flops 2147483648 | bytes 8388608 | tf_op jit(solution)/shard_map/pallas_call | solution.py:226
  184.2 42.3 %reduce-scatter.2.cloned.1.call-done = bf16[1,64,768]{2,1,0:T(8,128)(2,1)} async-done(((bf16[16,64,768]{2,1,0:T(8,128)(2,1)}), bf16[1,64,768]{2,1,0:T(8,128)(2,1)}) %reduce-scatter.2.cloned.1.call-update) | async-done | bytes 98320 | tf_op jit(solution)/shard_map/reduce_scatter | solution.py:268
  226.5 1.6 bitcast_convert_fusion
  228.1 0.0 all-to-all-done.1
  228.1 2.4 reduce_sum.21
  230.4 0.8 copy.39
  (1 shorter events, 0.0 us)
Async XLA Ops:
  7.2 15.6 %copy-start = (bf16[1024,768]{1,0:T(8,128)(2,1)S(1)}, bf16[1024,768]{1,0:T(8,128)(2,1)}, u32[]{:S(2)}) copy-start(bf16[1024,768]{1,0:T(8,128)(2,1)} %param.6) | copy-start | bytes 4718596
  12.6 87.3 %all-to-all-start = ((bf16[16,144,768]{2,1,0:T(8,128)(2,1)}), bf16[16,144,768]{2,1,0:T(8,128)(2,1)}, u32[]{:S(2)}, u32[]{:S(2)}) async-start(bf16[16,144,768]{2,1,0:T(8,128)(2,1)} %broadcast_in_dim.23), calls=%async_computation | async-start | bytes 7077888 | tf_op jit(solution)/shard_map/all_to_all | solution.py:255
  22.7 77.1 %all-gather.3.cloned.1.call-start = ((), (), s32[]{:S(2)}) async-start(), calls=%async_computation.5 | async-start | bytes 1671168 | tf_op jit(solution)/shard_map/all_gather | solution.py:247
  99.8 4.8 %copy-start.1 = (bf16[1024,768]{1,0:T(8,128)(2,1)S(1)}, bf16[1024,768]{1,0:T(8,128)(2,1)}, u32[]{:S(2)}) copy-start(bf16[1024,768]{1,0:T(8,128)(2,1)} %all-gather.3.cloned.1.call-done.w_ref) | copy-start | bytes 4718596
  99.8 13.3 %collective-permute-start = (bf16[16,144,768]{2,1,0:T(8,128)(2,1)}, bf16[16,144,768]{2,1,0:T(8,128)(2,1)}, u32[]{:S(2)}, u32[]{:S(2)}) collective-permute-start(bf16[16,144,768]{2,1,0:T(8,128)(2,1)} %all-to-all-done.x_ref.xa_ref), channel_id=1, source_target_pairs={{0,1},{1,0},{2,3},{3,2},{4,5},{5,4},{6,7},{7,6},{8,9},{9,8},{10,11... | collective-permute-start | bytes 10616840 | tf_op jit(solution)/shard_map/ppermute | solution.py:259
  113.1 8.5 %copy-start.2 = (bf16[1024,768]{0,1:T(8,128)(2,1)S(1)}, bf16[1024,768]{0,1:T(8,128)(2,1)}, u32[]{:S(2)}) copy-start(bf16[1024,768]{0,1:T(8,128)(2,1)} %copy.33) | copy-start | bytes 4718596
  128.3 35.0 %collective-permute-start.1 = (bf16[16,768,128]{2,1,0:T(8,128)(2,1)}, bf16[16,768,128]{2,1,0:T(8,128)(2,1)}, u32[]{:S(2)}, u32[]{:S(2)}) collective-permute-start(bf16[16,768,128]{2,1,0:T(8,128)(2,1)} %shard_map.77), channel_id=1, source_target_pairs={{0,1},{1,0},{2,3},{3,2},{4,5},{5,4},{6,7},{7,6},{8,9},{9,8},{10,11... | collective-permute-start | bytes 9437192 | tf_op jit(solution)/shard_map/ppermute | solution.py:264
  130.7 6.0 %collective-permute-start.2 = (bf16[16,128,128]{2,1,0:T(8,128)(2,1)S(1)}, bf16[16,128,128]{2,1,0:T(8,128)(2,1)S(1)}, u32[]{:S(2)}, u32[]{:S(2)}) collective-permute-start(bf16[16,128,128]{2,1,0:T(8,128)(2,1)S(1)} %get-tuple-element.22), channel_id=1, source_target_pairs={{0,1},{1,0},{2,3},{3,2},{4,5},{5,4},{6,7},{7,6},{8,9},{9,8},{10,11... | collective-permute-start | bytes 1572872 | tf_op jit(solution)/shard_map/ppermute | solution.py:265
  137.9 29.7 %all-to-all-start.2 = ((bf16[16,256,128]{2,1,0:T(8,128)(2,1)}), bf16[16,256,128]{2,1,0:T(8,128)(2,1)}, u32[]{:S(2)}, u32[]{:S(2)}) async-start(bf16[16,256,128]{2,1,0:T(8,128)(2,1)} %pad_maximum_fusion), calls=%async_computation.3 | async-start | bytes 2097152 | tf_op jit(solution)/shard_map/all_to_all | solution.py:272
  145.2 12.6 %copy-start.3 = (bf16[1024,768]{0,1:T(8,128)(2,1)S(1)}, bf16[1024,768]{0,1:T(8,128)(2,1)}, u32[]{:S(2)}) copy-start(bf16[1024,768]{0,1:T(8,128)(2,1)} %copy.33) | copy-start | bytes 4718596
  145.2 81.3 %reduce-scatter.2.cloned.1.call-start = ((), (), s32[]{:S(2)}) async-start(), calls=%async_computation.4 | async-start | bytes 1671168 | tf_op jit(solution)/shard_map/reduce_scatter | solution.py:268
  156.6 1.2 copy-start.4
  167.6 7.4 %copy-start.5 = (s32[128,16]{0,1:T(8,128)S(1)}, s32[128,16]{0,1:T(8,128)}, u32[]{:S(2)}) copy-start(s32[128,16]{0,1:T(8,128)} %param.7) | copy-start | bytes 24580
  167.7 60.4 %all-to-all-start.1 = ((bf16[16,768,128]{2,1,0:T(8,128)(2,1)}), bf16[16,768,128]{2,1,0:T(8,128)(2,1)}, u32[]{:S(2)}, u32[]{:S(2)}) async-start(bf16[16,768,128]{2,1,0:T(8,128)(2,1)} %add_convert_fusion), calls=%async_computation.1 | async-start | bytes 6291456 | tf_op jit(solution)/shard_map/all_to_all | solution.py:274
Sparse Core Ops, SparseCore 0:
  26.2 73.5 all-gather.2
  157.9 68.5 reduce-scatter.1

commit v4 on v3

--- a/solution.py
+++ b/solution.py
@@ -30,7 +30,9 @@
     offset = (meta[1] * HALF + 2).astype(F32)
     n = STEP * ROWS
     x = x_ref[:, :ROWS, :].reshape(n, D)
-    wanted = lax.broadcasted_iota(jnp.int32, (Z, ROWS), 0).astype(F32) * 16.0 + base
+    local = lax.broadcasted_iota(jnp.int32, (Z, ROWS), 0)
+    chunk = (local & 12) + ((local + meta[2]) & 3)
+    wanted = chunk.astype(F32) * 16.0 + base
     before = (
         lax.broadcasted_iota(jnp.int32, (ROWS, ROWS), 0)
         < lax.broadcasted_iota(jnp.int32, (ROWS, ROWS), 1)
@@ -117,84 +119,90 @@
     )(meta, rows, w)
 
 
-def weight_body(ga_ref, xa_ref, gb_ref, xb_ref, out_ref, acc):
-    step, half = pl.program_id(0), pl.num_programs(0) // 2
-
-    def add(g_ref, x_ref):
-        x = x_ref[:, :ROWS, :].reshape(-1, D)
-        for q in range(4):
-            rows = slice(q * 256, (q + 1) * 256)
-            acc[rows, :] += jnp.dot(g_ref[rows, :], x, preferred_element_type=F32)
+def weight_body(first, *refs):
+    if first:
+        g_ref, x_ref, out_ref, acc = refs
+    else:
+        g_ref, x_ref, in_ref, out_ref, acc = refs
+    step = pl.program_id(0)
 
     @pl.when(step == 0)
     def _():
-        acc[...] = jnp.zeros_like(acc)
-
-    @pl.when(step < half)
-    def _():
-        add(ga_ref, xa_ref)
-
-    @pl.when(step >= half)
-    def _():
-        add(gb_ref, xb_ref)
+        acc[...] = jnp.zeros_like(acc) if first else in_ref[...]
+
+    x = x_ref[:, :ROWS, :].reshape(-1, D)
+    for q in range(4):
+        rows = slice(q * 256, (q + 1) * 256)
+        acc[rows, :] += jnp.dot(g_ref[rows, :], x, preferred_element_type=F32)
 
     @pl.when(step == pl.num_programs(0) - 1)
     def _():
-        out_ref[...] = acc[...].astype(BF16)
-
-
-def weight_grad(ga, xa, gb, xb):
-    count, block = xa.shape[0], 8
-    half = count // block
-    low = lambda i: jnp.minimum(i, half - 1)
-    high = lambda i: jnp.maximum(i - half, 0)
+        out_ref[...] = acc[...].astype(out_ref.dtype)
+
+
+def weight_grad(g, x, total=None):
+    first = total is None
+    count, block = x.shape[0], 8
+    whole = pl.BlockSpec((COLS, D), lambda i: (0, 0))
     return pl.pallas_call(
-        weight_body,
-        grid=(2 * half,),
+        functools.partial(weight_body, first),
+        grid=(count // block,),
         in_specs=[
-            pl.BlockSpec((COLS, block * ROWS), lambda i: (0, low(i))),
-            pl.BlockSpec((block, ROWS + META, D), lambda i: (low(i), 0, 0)),
-            pl.BlockSpec((COLS, block * ROWS), lambda i: (0, high(i))),
-            pl.BlockSpec((block, ROWS + META, D), lambda i: (high(i), 0, 0)),
-        ],
-        out_specs=pl.BlockSpec((COLS, D), lambda i: (0, 0)),
-        out_shape=jax.ShapeDtypeStruct((COLS, D), BF16),
+            pl.BlockSpec((COLS, block * ROWS), lambda i: (0, i)),
+            pl.BlockSpec((block, ROWS + META, D), lambda i: (i, 0, 0)),
+        ]
+        + ([] if first else [whole]),
+        out_specs=whole,
+        out_shape=jax.ShapeDtypeStruct((COLS, D), F32 if first else BF16),
         scratch_shapes=[pltpu.VMEM((COLS, D), F32)],
         compiler_params=pltpu.CompilerParams(vmem_limit_bytes=VMEM),
         cost_estimate=pl.CostEstimate(
-            flops=4 * count * ROWS * COLS * D, bytes_accessed=18 * 2**20, transcendentals=0
-        ),
-    )(ga, xa, gb, xb)
-
-
-def row_body(wt_ref, g_ref, out_ref):
+            flops=2 * count * ROWS * COLS * D, bytes_accessed=12 * 2**20, transcendentals=0
+        ),
+    )(g, x, *([] if first else [total]))
+
+
+def row_body(first, wt_ref, g_ref, pack_ref, *refs):
+    if first:
+        (out_ref,) = refs
+    else:
+        back_ref, out_ref = refs
     for q in range(D // 256):
-        back = jnp.dot(
-            wt_ref[q * 256 : (q + 1) * 256, :], g_ref[...], preferred_element_type=F32
-        ).astype(BF16)
+        rows = slice(q * 256, (q + 1) * 256)
+        mine = jnp.dot(wt_ref[rows, :], g_ref[...], preferred_element_type=F32)
         for d in range(STEP):
-            out_ref[d, q * 256 : (q + 1) * 256, :] = back[:, d * ROWS : (d + 1) * ROWS]
-
-
-def row_grad(wt, g):
+            part = mine[:, d * ROWS : (d + 1) * ROWS]
+            if not first:
+                part = part + back_ref[d, rows, :].astype(F32)
+            out_ref[d, rows, :] = part.astype(BF16)
+    out_ref[:, D : D + BS, :] = pack_ref[...]
+    if not first:
+        out_ref[:, D + BS :, :] = back_ref[:, D:, :]
+
+
+def row_grad(wt, g, pack, back=None):
+    first = back is None
     count = g.shape[1] // ROWS
+    height = D + BS if first else D + 2 * BS
     return pl.pallas_call(
-        row_body,
+        functools.partial(row_body, first),
         grid=(count // STEP,),
         in_specs=[
             pl.BlockSpec((D, COLS), lambda i: (0, 0)),
             pl.BlockSpec((COLS, STEP * ROWS), lambda i: (0, i)),
-        ],
-        out_specs=pl.BlockSpec((STEP, D, ROWS), lambda i: (i, 0, 0)),
-        out_shape=jax.ShapeDtypeStruct((count, D, ROWS), BF16),
+            pl.BlockSpec((STEP, BS, ROWS), lambda i: (i, 0, 0)),
+        ]
+        + ([] if first else [pl.BlockSpec((STEP, D + BS, ROWS), lambda i: (i, 0, 0))]),
+        out_specs=pl.BlockSpec((STEP, height, ROWS), lambda i: (i, 0, 0)),
+        out_shape=jax.ShapeDtypeStruct((count, height, ROWS), BF16),
         compiler_params=pltpu.CompilerParams(vmem_limit_bytes=VMEM),
         cost_estimate=pl.CostEstimate(
-            flops=2 * count * ROWS * COLS * D, bytes_accessed=9 * 2**20, transcendentals=0
-        ),
-    )(wt, g)
-
-
-def unpack_body(key_ref, got_ref, out_ref):
+            flops=2 * count * ROWS * COLS * D, bytes_accessed=12 * 2**20, transcendentals=0
+        ),
+    )(wt, g, pack, *([] if first else [back]))
+
+
+def finish_body(key_ref, rows_ref, pack_ref, gx_ref, out_ref):
     key = key_ref[...]
     lane = lax.broadcasted_iota(jnp.int32, (1, 2 * ROWS), 1)
     total = jnp.zeros(out_ref.shape, F32)
@@ -206,7 +214,7 @@
                 [
                     jnp.concatenate(
                         [
-                            got_ref[2 * owner + h, base + hh * HALF : base + (hh + 1) * HALF, :]
+                            pack_ref[2 * owner + h, base + hh * HALF : base + (hh + 1) * HALF, :]
                             for hh in range(2)
                         ],
                         axis=1,
@@ -218,61 +226,94 @@
             pick = jnp.where(key == lane + chunk * 2 * ROWS, 1.0, 0.0).astype(BF16)
             total += lax.dot_general(pick, table, NT, preferred_element_type=F32)
     out_ref[...] = total.astype(BF16)
-
-
-def unpack(key, got):
-    pairs = key.shape[0]
-    block = 512
+    for q in range(3):
+        rows = slice(q * ROWS, (q + 1) * ROWS)
+        part = rows_ref[0, rows, :].astype(F32)
+        for i in range(1, 16):
+            part = part + rows_ref[i, rows, :].astype(F32)
+        gx_ref[:, rows] = part.T.astype(BF16)
+
+
+def finish(key, got):
+    pairs, block, deep = key.shape[0], 1024, D // 2
     return pl.pallas_call(
-        unpack_body,
-        grid=(pairs // block,),
+        finish_body,
+        grid=(2,),
         in_specs=[
             pl.BlockSpec((block, 2 * ROWS), lambda i: (i, 0)),
-            pl.BlockSpec(got.shape, lambda i: (0, 0, 0)),
+            pl.BlockSpec((16, deep, ROWS), lambda i: (0, i, 0)),
+            pl.BlockSpec((16, 2 * BS, ROWS), lambda i: (0, 3, 0)),
         ],
-        out_specs=pl.BlockSpec((block, BS), lambda i: (i, 0)),
-        out_shape=jax.ShapeDtypeStruct((pairs, BS), BF16),
+        out_specs=[
+            pl.BlockSpec((ROWS, deep), lambda i: (0, i)),
+            pl.BlockSpec((block, BS), lambda i: (i, 0)),
+        ],
+        out_shape=[
+            jax.ShapeDtypeStruct((ROWS, D), BF16),
+            jax.ShapeDtypeStruct((pairs, BS), BF16),
+        ],
         compiler_params=pltpu.CompilerParams(vmem_limit_bytes=VMEM),
         cost_estimate=pl.CostEstimate(
             flops=2 * pairs * 4096 * BS, bytes_accessed=8 * 2**20, transcendentals=0
         ),
-    )(key, got)
+    )(key, got, got)
+
+
+def shift(x, k):
+    return lax.ppermute(x, ("zhi", "zlo"), [(s, (s - k) % Z) for s in range(Z)])
+
+
+def gather_z(mine):
+    half = HALF // 2
+    copies = jnp.broadcast_to(mine[None], (4,) + mine.shape)
+    every = lax.all_to_all(copies, "zhi", split_axis=0, concat_axis=0, tiled=True)
+    one, last = shift(every, 1), shift(every, -1)
+    low, high = shift(every[:, :half], 2), shift(every[:, half:], -2)
+    return jnp.stack([every, one, jnp.concatenate([low, high], axis=1), last], axis=1)
+
+
+def reduce_z(total, after):
+    half = HALF // 2
+    total = total.reshape(4, 4, HALF, D)
+    one, last = shift(total[:, 1], -1), shift(total[:, 3], 1)
+    low, high = shift(total[:, 2, :half], -2), shift(total[:, 2, half:], 2)
+    every = total[:, 0].astype(F32) + one.astype(F32) + last.astype(F32)
+    every = (every + jnp.concatenate([low, high], axis=1).astype(F32)).astype(BF16)
+    every, after = lax.optimization_barrier((every, after))
+    got = lax.all_to_all(every, "zhi", split_axis=0, concat_axis=0, tiled=True)
+    return jnp.sum(got, axis=0, dtype=F32), after
 
 
 def shards(features, weights, block_ids, label_codes, counts):
     inst = lax.axis_index(PLANE)
     core = lax.axis_index("core")
-    meta = jnp.stack([8 * core + inst // 2, inst % 2]).astype(jnp.int32)
+    depth = lax.axis_index("zlo")
+    meta = jnp.stack([8 * core + inst // 2, inst % 2, depth]).astype(jnp.int32)
     mine = lax.dynamic_slice_in_dim(weights, inst * HALF, HALF, 0)
-    w = lax.all_gather(mine, "z").reshape(COLS, D)
+    w = gather_z(mine).reshape(COLS, D)
 
     alive = jnp.arange(TOP, dtype=jnp.int32)[None, :] < counts[:, None]
     code = jnp.where(alive, jnp.minimum(label_codes, BS) + 2, 1)
     slots = jnp.concatenate([block_ids.T, code.T], axis=1).astype(BF16)
     slots = jnp.pad(slots, ((0, 0), (0, D - 2 * ROWS)))
     sent = jnp.concatenate([features, slots], axis=0)
-    copies = jnp.broadcast_to(sent[None], (Z,) + sent.shape)
+    copies = jnp.broadcast_to(sent[None], (16,) + sent.shape)
     own = lax.all_to_all(copies, PLANE, split_axis=0, concat_axis=0, tiled=True)
     swap = [(0, 1), (1, 0)]
     own, w = lax.optimization_barrier((own, w))
     wt = w.T
     other = lax.ppermute(own, "core", swap)
     own_grad, own_pack = expert(meta, own, w)
+    other, own_grad = lax.optimization_barrier((other, own_grad))
     other_grad, other_pack = expert(meta, other, w)
-    other_rows = row_grad(wt, other_grad)
-    other_rows, own_grad = lax.optimization_barrier((other_rows, own_grad))
-    back_rows = lax.ppermute(other_rows, "core", swap)
-    back_pack = lax.ppermute(other_pack, "core", swap)
-    total = weight_grad(own_grad, own, other_grad, other)
+    other_out = row_grad(wt, other_grad, other_pack)
+    back = lax.ppermute(other_out, "core", swap)
+    other_out, other_grad = lax.optimization_barrier((other_out, other_grad))
+    total = weight_grad(other_grad, other)
     total, own_grad = lax.optimization_barrier((total, own_grad))
-    grad_w = lax.psum_scatter(
-        total.reshape(Z, HALF, D), "z", scatter_dimension=0, tiled=False
-    ).astype(F32)
-    packs = jnp.concatenate([own_pack, back_pack], axis=1)
-    got = lax.all_to_all(packs, PLANE, split_axis=0, concat_axis=0, tiled=True)
-    sums = (row_grad(wt, own_grad).astype(F32) + back_rows.astype(F32)).astype(BF16)
-    got_rows = lax.all_to_all(sums, PLANE, split_axis=0, concat_axis=0, tiled=True)
-    grad_x = jnp.sum(got_rows, axis=0, dtype=F32).T.astype(BF16)
+    payload = row_grad(wt, own_grad, own_pack, back)
+    got = lax.all_to_all(payload, PLANE, split_axis=0, concat_axis=0, tiled=True)
+    payload, own_grad = lax.optimization_barrier((payload, own_grad))
 
     blocks = jnp.arange(256, dtype=jnp.int32)
     named = (block_ids[:, :, None] == blocks).any(axis=1).astype(BF16)
@@ -282,27 +323,30 @@
     rank = jnp.sum(jnp.where(block_ids[:, :, None] == blocks, rank[:, None, :], 0.0), axis=2)
     rank = rank.astype(jnp.int32)
     row = block_ids // 16
+    row = (row & 12) + ((row - depth) & 3)
     owner = block_ids % 16
     crossed = (owner // 8) ^ core
     key = (((owner % 8) * 2 + crossed) * 2 + row // 8) * ROWS + (row % 8) * MOST + rank
+    grad_w, key = reduce_z(weight_grad(own_grad, own, total), key)
     key = jnp.broadcast_to(key.reshape(-1, 1), (ROWS * TOP, 2 * ROWS))
-    grad_logits = unpack(key, got).reshape(ROWS, TOP, BS)
+    grad_x, grad_logits = finish(key, got)
+    grad_logits = grad_logits.reshape(ROWS, TOP, BS)
     return (grad_x, grad_w, grad_logits)
 
 
 def solution(mesh):
-    mesh = Mesh(mesh.devices.reshape(4, 4, Z, 2), ("y", "x", "z", "core"))
-    everywhere = ("y", "x", "z", "core")
+    axes = ("y", "x", "zhi", "zlo", "core")
+    mesh = Mesh(mesh.devices.reshape(4, 4, 4, 4, 2), axes)
     in_specs = (
-        P(everywhere, None),
-        P(("z", "core"), None),
-        P(everywhere, None),
-        P(everywhere, None),
-        P(everywhere),
+        P(axes, None),
+        P(axes[2:], None),
+        P(axes, None),
+        P(axes, None),
+        P(axes),
     )
     out_specs = (
-        P(everywhere, None),
-        P(("z", "core", "y", "x"), None),
-        P(everywhere, None, None),
+        P(axes, None),
+        P(axes[2:] + PLANE, None),
+        P(axes, None, None),
     )
     return jax.shard_map(shards, mesh=mesh, in_specs=in_specs, out_specs=out_specs, check_vma=False)

time: 239 us -> 281 us (1.18)
  the two profiles are of different devices: /device:TPU:2 before, /device:TPU:128 now
where the time goes in v4:
time: 281 us; the launch traced here: 280 us
  waiting for transfers between devices  118 us (42%)
  starting transfers between devices  66.5 us (24%)
  Pallas kernels  51.2 us (18%)
  blocking collectives  29.7 us (11%)
  local copies, waits for them, and re-layouts  8.18 us (3%)
  other arithmetic  5.18 us (2%)
    all_to_all x1, waiting for transfers between devices, shards(): lax.all_to_all(payload, PLANE, split_axis=0, concat_axis=0, tiled=True)  62.6 us
    ppermute x8, starting transfers between devices, shift(): return lax.ppermute(x, ('zhi', 'zlo'), [(s, (s - k) % Z) for s in range(Z)])  36.5 us
    all_to_all x1, blocking collectives, reduce_z(): got = lax.all_to_all(every, 'zhi', split_axis=0, concat_axis=0, tiled=True)  29.7 us
    all_to_all x1, waiting for transfers between devices, gather_z(): lax.all_to_all(copies, 'zhi', split_axis=0, concat_axis=0, tiled=True)  19.3 us
    all_to_all x1, waiting for transfers between devices, shards(): own = lax.all_to_all(copies, PLANE, split_axis=0, concat_axis=0, tiled=True)  19.1 us
    ppermute x8, waiting for transfers between devices, shift(): return lax.ppermute(x, ('zhi', 'zlo'), [(s, (s - k) % Z) for s in range(Z)])  17.4 us
    pallas_call x2, Pallas kernels, expert(): pl.pallas_call(expert_body, grid_spec=pltpu.PrefetchScalarGridSpec(num_sc...  17.1 us
    pallas_call x2, Pallas kernels, row_grad(): pl.pallas_call(functools.partial(row_body, first), grid=(count // STEP,),...  14.3 us
  transfers between devices with their start and end apart: 13, of which 6 were waited for; matrix products, arithmetic and copies ran while one was open for 3% of the time, Pallas kernels for 5%

profile of v4, /device:TPU:128, one launch (start us, length us, event | category | flops | bytes accessed | tf_op | source)
XLA Modules:
  0.0 280.3 jit_solution(13903409216504348326)
XLA Ops:
  0.6 0.0 copy-start
  0.7 1.4 copy-done
  2.1 0.8 broadcast_in_dim.22
  2.8 13.8 %all-to-all-start.1 = ((bf16[4,64,768]{2,1,0:T(8,128)(2,1)}), bf16[4,64,768]{2,1,0:T(8,128)(2,1)S(1)}, u32[]{:S(2)}, u32[]{:S(2)}) async-start(bf16[4,64,768]{2,1,0:T(8,128)(2,1)} %broadcast_in_dim.22), calls=%async_computation.1 | async-start | bytes 786432 | tf_op jit(solution)/shard_map/all_to_all | solution.py:269
  16.6 0.8 copy.41
  17.4 0.7 fusion.26
  18.2 0.1 copy.42
  18.2 0.7 convert_bitcast_fusion
  19.0 0.9 pad_maximum_fusion.1
  19.9 19.3 %all-to-all-done.1 = bf16[4,64,768]{2,1,0:T(8,128)(2,1)S(1)} async-done(((bf16[4,64,768]{2,1,0:T(8,128)(2,1)}), bf16[4,64,768]{2,1,0:T(8,128)(2,1)S(1)}, u32[]{:S(2)}, u32[]{:S(2)}) %all-to-all-start.1) | async-done | bytes 393248 | tf_op jit(solution)/shard_map/all_to_all | solution.py:269
  39.2 2.0 broadcast_in_dim.21
  41.2 7.1 %all-to-all-start = ((bf16[16,144,768]{2,1,0:T(8,128)(2,1)}), bf16[16,144,768]{2,1,0:T(8,128)(2,1)}, u32[]{:S(2)}, u32[]{:S(2)}) async-start(bf16[16,144,768]{2,1,0:T(8,128)(2,1)} %broadcast_in_dim.21), calls=%async_computation | async-start | bytes 7077888 | tf_op jit(solution)/shard_map/all_to_all | solution.py:301
  48.3 2.4 collective-permute-start.3
  50.7 4.6 %collective-permute-start = (bf16[4,64,768]{2,1,0:T(8,128)(2,1)S(1)}, bf16[4,64,768]{2,1,0:T(8,128)(2,1)S(1)}, u32[]{:S(2)}, u32[]{:S(2)}) collective-permute-start(bf16[4,64,768]{2,1,0:T(8,128)(2,1)S(1)} %all-to-all-done.1), channel_id=1, source_target_pairs={{0,30},{2,0},{4,2},{6,4},{8,6},{10,8},{12,10},{14,12},{16,14},{18,... | collective-permute-start | bytes 1179656 | tf_op jit(solution)/shard_map/ppermute | solution.py:263
  55.4 1.9 collective-permute-start.2
  57.3 6.0 %collective-permute-start.1 = (bf16[4,32,768]{2,1,0:T(8,128)(2,1)S(1)}, bf16[4,32,768]{2,1,0:T(8,128)(2,1)S(1)}, u32[]{:S(2)}, u32[]{:S(2)}) collective-permute-start(bf16[4,32,768]{2,1,0:T(8,128)(2,1)S(1)} %get-tuple-element.39), channel_id=1, source_target_pairs={{0,28},{2,30},{4,0},{6,2},{8,4},{10,6},{12,8},{14,10},{16,12},{18,... | collective-permute-start | bytes 589832 | tf_op jit(solution)/shard_map/ppermute | solution.py:263
  63.4 4.7 %collective-permute-done.2 = bf16[4,32,768]{2,1,0:T(8,128)(2,1)S(1)} collective-permute-done((bf16[4,32,768]{2,1,0:T(8,128)(2,1)S(1)}, bf16[4,32,768]{2,1,0:T(8,128)(2,1)S(1)}, u32[]{:S(2)}, u32[]{:S(2)}) %collective-permute-start.2) | collective-permute-done | bytes 196640 | tf_op jit(solution)/shard_map/ppermute | solution.py:263
  68.0 2.8 collective-permute-done.1
  70.9 0.0 collective-permute-done.3
  70.9 0.0 collective-permute-done
  70.9 0.2 pad_maximum_fusion
  71.1 0.1 copy.43
  71.2 19.1 %all-to-all-done.x_ref.refs_1_ = bf16[16,144,768]{2,1,0:T(8,128)(2,1)} async-done(((bf16[16,144,768]{2,1,0:T(8,128)(2,1)}), bf16[16,144,768]{2,1,0:T(8,128)(2,1)}, u32[]{:S(2)}, u32[]{:S(2)}) %all-to-all-start) | async-done | bytes 3538976 | tf_op jit(solution)/shard_map/all_to_all | solution.py:301
  90.3 1.9 collective-permute-start.4
  92.2 0.1 pad_add_fusion.meta
  92.3 1.6 copy.44
  93.9 8.5 %shard_map.76 = (bf16[1024,2048]{1,0:T(8,128)(2,1)}, bf16[16,128,128]{2,1,0:T(8,128)(2,1)S(1)}) custom-call(s32[3]{0:T(128)S(1)} %pad_add_fusion.meta, bf16[16,144,768]{2,1,0:T(8,128)(2,1)} %all-to-all-done.x_ref.refs_1_, bf16[1024,768]{1,0:T(8,128)(2,1)S(1)} %bitcast.39), custom_call_target="tpu_custom_call" | custom-call | flops 3221225472 | bytes 10485760 | tf_op jit(solution)/shard_map/pallas_call | solution.py:95
  102.5 0.8 copy-done.3
  103.3 0.0 collective-permute-done.4.x_ref.refs_1_
  103.3 8.5 %shard_map.77 = (bf16[1024,2048]{1,0:T(8,128)(2,1)}, bf16[16,128,128]{2,1,0:T(8,128)(2,1)S(1)}) custom-call(s32[3]{0:T(128)S(1)} %pad_add_fusion.meta, bf16[16,144,768]{2,1,0:T(8,128)(2,1)} %collective-permute-done.4.x_ref.refs_1_, bf16[1024,768]{1,0:T(8,128)(2,1)S(1)} %bitcast.40), custom_call_target="tpu_custom_call" | custom-call | flops 3221225472 | bytes 10485760 | tf_op jit(solution)/shard_map/pallas_call | solution.py:95
  111.8 0.0 copy-done.1
  111.8 6.8 %shard_map.78 = bf16[16,896,128]{2,1,0:T(8,128)(2,1)} custom-call(bf16[768,1024]{1,0:T(8,128)(2,1)S(1)} %bitcast.44, bf16[1024,2048]{1,0:T(8,128)(2,1)} %get-tuple-element.25.g_ref.refs_0_, bf16[16,128,128]{2,1,0:T(8,128)(2,1)S(1)} %get-tuple-element.24.pack_ref), custom_call_target="tpu_custom_call" | custom-call | flops 3221225472 | bytes 12582912 | tf_op jit(solution)/shard_map/pallas_call | solution.py:187
  118.6 2.4 collective-permute-start.5
  121.0 0.0 copy-done.5
  121.0 0.1 copy.49
  121.1 0.6 fusion
  121.7 0.2 fusion.22
  121.8 0.7 select_reduce_fusion
  122.6 0.0 copy-start.2
  122.6 0.0 copy-start.4
  122.6 6.3 %shard_map.79.refs_2_ = f32[1024,768]{1,0:T(8,128)S(1)} custom-call(bf16[1024,2048]{1,0:T(8,128)(2,1)} %get-tuple-element.25.g_ref.refs_0_, bf16[16,144,768]{2,1,0:T(8,128)(2,1)} %collective-permute-done.4.x_ref.refs_1_), custom_call_target="tpu_custom_call" | custom-call | flops 3221225472 | bytes 12582912 | tf_op jit(solution)/shard_map/pallas_call | solution.py:147
  128.9 0.0 collective-permute-done.5.refs_0_
  128.9 0.0 copy-done.2
  128.9 0.0 copy-done.4
  128.9 7.6 %shard_map.80 = bf16[16,1024,128]{2,1,0:T(8,128)(2,1)} custom-call(bf16[768,1024]{1,0:T(8,128)(2,1)S(1)} %bitcast.45, bf16[1024,2048]{1,0:T(8,128)(2,1)} %get-tuple-element.29.g_ref.refs_0_, bf16[16,128,128]{2,1,0:T(8,128)(2,1)S(1)} %copy-done.4, bf16[16,896,128]{2,1,0:T(8,128)(2,1)} %collective-permute-done.5.refs_0_), custom_call_target="tpu_custom_call" | custom-call | flops 3221225472 | bytes 12582912 | tf_op jit(solution)/shard_map/pallas_call | solution.py:187
  136.5 6.1 %shard_map.81 = bf16[1024,768]{1,0:T(8,128)(2,1)S(1)} custom-call(bf16[1024,2048]{1,0:T(8,128)(2,1)} %get-tuple-element.29.g_ref.refs_0_, bf16[16,144,768]{2,1,0:T(8,128)(2,1)} %all-to-all-done.x_ref.refs_1_, f32[1024,768]{1,0:T(8,128)S(1)} %shard_map.79.refs_2_), custom_call_target="tpu_custom_call" | custom-call | flops 3221225472 | bytes 12582912 | tf_op jit(solution)/shard_map/pallas_call | solution.py:147
  142.6 0.1 slice_bitcast_fusion.1
  142.7 9.1 %collective-permute-start.7 = (bf16[4,64,768]{2,1,0:T(8,128)(2,1)S(1)}, bf16[4,64,768]{2,1,0:T(8,128)(2,1)S(1)}, u32[]{:S(2)}, u32[]{:S(2)}) collective-permute-start(bf16[4,64,768]{2,1,0:T(8,128)(2,1)S(1)} %get-tuple-element.38), channel_id=1, source_target_pairs={{0,30},{2,0},{4,2},{6,4},{8,6},{10,8},{12,10},{14,12},{16,14},{18,... | collective-permute-start | bytes 1179656 | tf_op jit(solution)/shard_map/ppermute | solution.py:263
  151.7 5.7 %collective-permute-start.6 = (bf16[4,64,768]{2,1,0:T(8,128)(2,1)S(1)}, bf16[4,64,768]{2,1,0:T(8,128)(2,1)S(1)}, u32[]{:S(2)}, u32[]{:S(2)}) collective-permute-start(bf16[4,64,768]{2,1,0:T(8,128)(2,1)S(1)} %get-tuple-element.37), channel_id=1, source_target_pairs={{0,2},{2,4},{4,6},{6,8},{8,10},{10,12},{12,14},{14,16},{16,18},{18... | collective-permute-start | bytes 1179656 | tf_op jit(solution)/shard_map/ppermute | solution.py:263
  157.5 2.9 %collective-permute-start.9 = (bf16[4,32,768]{2,1,0:T(8,128)(2,1)S(1)}, bf16[4,32,768]{2,1,0:T(8,128)(2,1)S(1)}, u32[]{:S(2)}, u32[]{:S(2)}) collective-permute-start(bf16[4,32,768]{2,1,0:T(8,128)(2,1)S(1)} %get-tuple-element.36), channel_id=1, source_target_pairs={{0,28},{2,30},{4,0},{6,2},{8,4},{10,6},{12,8},{14,10},{16,12},{18,... | collective-permute-start | bytes 589832 | tf_op jit(solution)/shard_map/ppermute | solution.py:263
  160.5 3.8 %collective-permute-start.8 = (bf16[4,32,768]{2,1,0:T(8,128)(2,1)S(1)}, bf16[4,32,768]{2,1,0:T(8,128)(2,1)S(1)}, u32[]{:S(2)}, u32[]{:S(2)}) collective-permute-start(bf16[4,32,768]{2,1,0:T(8,128)(2,1)S(1)} %get-tuple-element.35), channel_id=1, source_target_pairs={{0,4},{2,6},{4,8},{6,10},{8,12},{10,14},{12,16},{14,18},{16,20},{1... | collective-permute-start | bytes 589832 | tf_op jit(solution)/shard_map/ppermute | solution.py:263
  164.3 0.2 fusion.10
  164.5 9.9 %collective-permute-done.9 = bf16[4,32,768]{2,1,0:T(8,128)(2,1)S(1)} collective-permute-done((bf16[4,32,768]{2,1,0:T(8,128)(2,1)S(1)}, bf16[4,32,768]{2,1,0:T(8,128)(2,1)S(1)}, u32[]{:S(2)}, u32[]{:S(2)}) %collective-permute-start.9) | collective-permute-done | bytes 196640 | tf_op jit(solution)/shard_map/ppermute | solution.py:263
  174.4 0.0 collective-permute-done.8
  174.4 0.0 collective-permute-done.7
  174.4 0.0 collective-permute-done.6
  174.4 0.2 fusion.3
  174.6 29.7 %all_to_all.20 = bf16[4,64,768]{2,1,0:T(8,128)(2,1)S(1)} all-to-all(bf16[4,64,768]{2,1,0:T(8,128)(2,1)S(1)} %fusion.3), channel_id=1, replica_groups=mesh['y'=4,'x'=4,'zhi'=4,'zlo'=4,'core'=2] {'zhi'}, dimensions={0} | all-to-all | bytes 786432 | tf_op jit(solution)/shard_map/all_to_all | solution.py:283
  204.4 4.7 %all-to-all-start.2 = ((bf16[16,1024,128]{2,1,0:T(8,128)(2,1)}), bf16[16,1024,128]{2,1,0:T(8,128)(2,1)}, u32[]{:S(2)}, u32[]{:S(2)}) async-start(bf16[16,1024,128]{2,1,0:T(8,128)(2,1)} %shard_map.80), calls=%async_computation.2 | async-start | bytes 8388608 | tf_op jit(solution)/shard_map/all_to_all | solution.py:315
  209.1 0.1 broadcast_in_dim.29
  209.2 0.7 convert_reduce_fusion
  209.9 62.6 %all-to-all-done.2.rows_ref.pack_ref = bf16[16,1024,128]{2,1,0:T(8,128)(2,1)} async-done(((bf16[16,1024,128]{2,1,0:T(8,128)(2,1)}), bf16[16,1024,128]{2,1,0:T(8,128)(2,1)}, u32[]{:S(2)}, u32[]{:S(2)}) %all-to-all-start.2) | async-done | bytes 4194336 | tf_op jit(solution)/shard_map/all_to_all | solution.py:315
  272.5 0.3 broadcast_in_dim.50.key_ref
  272.9 7.4 %shard_map.82 = (bf16[128,768]{1,0:T(8,128)(2,1)}, bf16[2048,128]{1,0:T(8,128)(2,1)}) custom-call(s32[2048,256]{1,0:T(8,128)S(1)} %broadcast_in_dim.50.key_ref, bf16[16,1024,128]{2,1,0:T(8,128)(2,1)} %all-to-all-done.2.rows_ref.pack_ref, bf16[16,1024,128]{2,1,0:T(8,128)(2,1)} %all-to-all-done.2.rows_ref.pack_ref), custom_call_target="tpu_custom_call" | custom-call | flops 2147483648 | bytes 8388608 | tf_op jit(solution)/shard_map/pallas_call | solution.py:239
  (8 shorter events, 0.1 us)
Async XLA Ops:
  0.6 1.4 copy-start
  2.8 36.4 %all-to-all-start.1 = ((bf16[4,64,768]{2,1,0:T(8,128)(2,1)}), bf16[4,64,768]{2,1,0:T(8,128)(2,1)S(1)}, u32[]{:S(2)}, u32[]{:S(2)}) async-start(bf16[4,64,768]{2,1,0:T(8,128)(2,1)} %broadcast_in_dim.22), calls=%async_computation.1 | async-start | bytes 786432 | tf_op jit(solution)/shard_map/all_to_all | solution.py:269
  41.2 49.1 %all-to-all-start = ((bf16[16,144,768]{2,1,0:T(8,128)(2,1)}), bf16[16,144,768]{2,1,0:T(8,128)(2,1)}, u32[]{:S(2)}, u32[]{:S(2)}) async-start(bf16[16,144,768]{2,1,0:T(8,128)(2,1)} %broadcast_in_dim.21), calls=%async_computation | async-start | bytes 7077888 | tf_op jit(solution)/shard_map/all_to_all | solution.py:301
  48.3 22.6 %collective-permute-start.3 = (bf16[4,64,768]{2,1,0:T(8,128)(2,1)S(1)}, bf16[4,64,768]{2,1,0:T(8,128)(2,1)S(1)}, u32[]{:S(2)}, u32[]{:S(2)}) collective-permute-start(bf16[4,64,768]{2,1,0:T(8,128)(2,1)S(1)} %all-to-all-done.1), channel_id=1, source_target_pairs={{0,2},{2,4},{4,6},{6,8},{8,10},{10,12},{12,14},{14,16},{16,18},{18... | collective-permute-start | bytes 1179656 | tf_op jit(solution)/shard_map/ppermute | solution.py:263
  50.7 20.2 %collective-permute-start = (bf16[4,64,768]{2,1,0:T(8,128)(2,1)S(1)}, bf16[4,64,768]{2,1,0:T(8,128)(2,1)S(1)}, u32[]{:S(2)}, u32[]{:S(2)}) collective-permute-start(bf16[4,64,768]{2,1,0:T(8,128)(2,1)S(1)} %all-to-all-done.1), channel_id=1, source_target_pairs={{0,30},{2,0},{4,2},{6,4},{8,6},{10,8},{12,10},{14,12},{16,14},{18,... | collective-permute-start | bytes 1179656 | tf_op jit(solution)/shard_map/ppermute | solution.py:263
  55.4 12.6 %collective-permute-start.2 = (bf16[4,32,768]{2,1,0:T(8,128)(2,1)S(1)}, bf16[4,32,768]{2,1,0:T(8,128)(2,1)S(1)}, u32[]{:S(2)}, u32[]{:S(2)}) collective-permute-start(bf16[4,32,768]{2,1,0:T(8,128)(2,1)S(1)} %get-tuple-element.40), channel_id=1, source_target_pairs={{0,4},{2,6},{4,8},{6,10},{8,12},{10,14},{12,16},{14,18},{16,20},{1... | collective-permute-start | bytes 589832 | tf_op jit(solution)/shard_map/ppermute | solution.py:263
  57.3 13.5 %collective-permute-start.1 = (bf16[4,32,768]{2,1,0:T(8,128)(2,1)S(1)}, bf16[4,32,768]{2,1,0:T(8,128)(2,1)S(1)}, u32[]{:S(2)}, u32[]{:S(2)}) collective-permute-start(bf16[4,32,768]{2,1,0:T(8,128)(2,1)S(1)} %get-tuple-element.39), channel_id=1, source_target_pairs={{0,28},{2,30},{4,0},{6,2},{8,4},{10,6},{12,8},{14,10},{16,12},{18,... | collective-permute-start | bytes 589832 | tf_op jit(solution)/shard_map/ppermute | solution.py:263
  90.3 13.0 %collective-permute-start.4 = (bf16[16,144,768]{2,1,0:T(8,128)(2,1)}, bf16[16,144,768]{2,1,0:T(8,128)(2,1)}, u32[]{:S(2)}, u32[]{:S(2)}) collective-permute-start(bf16[16,144,768]{2,1,0:T(8,128)(2,1)} %all-to-all-done.x_ref.refs_1_), channel_id=1, source_target_pairs={{0,1},{1,0},{2,3},{3,2},{4,5},{5,4},{6,7},{7,6},{8,9},{9,8},{10,11... | collective-permute-start | bytes 10616840 | tf_op jit(solution)/shard_map/ppermute | solution.py:305
  102.5 0.8 copy-start.3
  103.3 8.5 %copy-start.1 = (bf16[1024,768]{0,1:T(8,128)(2,1)S(1)}, bf16[1024,768]{0,1:T(8,128)(2,1)}, u32[]{:S(2)}) copy-start(bf16[1024,768]{0,1:T(8,128)(2,1)} %copy.44) | copy-start | bytes 4718596
  111.8 9.2 %copy-start.5 = (s32[128,16]{0,1:T(8,128)S(1)}, s32[128,16]{0,1:T(8,128)}, u32[]{:S(2)}) copy-start(s32[128,16]{0,1:T(8,128)} %param.7) | copy-start | bytes 24580
  118.6 10.3 %collective-permute-start.5 = (bf16[16,896,128]{2,1,0:T(8,128)(2,1)}, bf16[16,896,128]{2,1,0:T(8,128)(2,1)}, u32[]{:S(2)}, u32[]{:S(2)}) collective-permute-start(bf16[16,896,128]{2,1,0:T(8,128)(2,1)} %shard_map.78), channel_id=1, source_target_pairs={{0,1},{1,0},{2,3},{3,2},{4,5},{5,4},{6,7},{7,6},{8,9},{9,8},{10,11... | collective-permute-start | bytes 11010056 | tf_op jit(solution)/shard_map/ppermute | solution.py:310
  122.6 6.3 %copy-start.2 = (bf16[1024,768]{0,1:T(8,128)(2,1)S(1)}, bf16[1024,768]{0,1:T(8,128)(2,1)}, u32[]{:S(2)}) copy-start(bf16[1024,768]{0,1:T(8,128)(2,1)} %copy.44) | copy-start | bytes 4718596
  122.6 6.3 %copy-start.4 = (bf16[16,128,128]{2,1,0:T(8,128)(2,1)S(1)}, bf16[16,128,128]{2,1,0:T(8,128)(2,1)}, u32[]{:S(2)}) copy-start(bf16[16,128,128]{2,1,0:T(8,128)(2,1)} %copy-done.3) | copy-start | bytes 1572868
  142.7 31.8 %collective-permute-start.7 = (bf16[4,64,768]{2,1,0:T(8,128)(2,1)S(1)}, bf16[4,64,768]{2,1,0:T(8,128)(2,1)S(1)}, u32[]{:S(2)}, u32[]{:S(2)}) collective-permute-start(bf16[4,64,768]{2,1,0:T(8,128)(2,1)S(1)} %get-tuple-element.38), channel_id=1, source_target_pairs={{0,30},{2,0},{4,2},{6,4},{8,6},{10,8},{12,10},{14,12},{16,14},{18,... | collective-permute-start | bytes 1179656 | tf_op jit(solution)/shard_map/ppermute | solution.py:263
  151.7 22.7 %collective-permute-start.6 = (bf16[4,64,768]{2,1,0:T(8,128)(2,1)S(1)}, bf16[4,64,768]{2,1,0:T(8,128)(2,1)S(1)}, u32[]{:S(2)}, u32[]{:S(2)}) collective-permute-start(bf16[4,64,768]{2,1,0:T(8,128)(2,1)S(1)} %get-tuple-element.37), channel_id=1, source_target_pairs={{0,2},{2,4},{4,6},{6,8},{8,10},{10,12},{12,14},{14,16},{16,18},{18... | collective-permute-start | bytes 1179656 | tf_op jit(solution)/shard_map/ppermute | solution.py:263
  157.5 16.9 %collective-permute-start.9 = (bf16[4,32,768]{2,1,0:T(8,128)(2,1)S(1)}, bf16[4,32,768]{2,1,0:T(8,128)(2,1)S(1)}, u32[]{:S(2)}, u32[]{:S(2)}) collective-permute-start(bf16[4,32,768]{2,1,0:T(8,128)(2,1)S(1)} %get-tuple-element.36), channel_id=1, source_target_pairs={{0,28},{2,30},{4,0},{6,2},{8,4},{10,6},{12,8},{14,10},{16,12},{18,... | collective-permute-start | bytes 589832 | tf_op jit(solution)/shard_map/ppermute | solution.py:263
  160.5 14.0 %collective-permute-start.8 = (bf16[4,32,768]{2,1,0:T(8,128)(2,1)S(1)}, bf16[4,32,768]{2,1,0:T(8,128)(2,1)S(1)}, u32[]{:S(2)}, u32[]{:S(2)}) collective-permute-start(bf16[4,32,768]{2,1,0:T(8,128)(2,1)S(1)} %get-tuple-element.35), channel_id=1, source_target_pairs={{0,4},{2,6},{4,8},{6,10},{8,12},{10,14},{12,16},{14,18},{16,20},{1... | collective-permute-start | bytes 589832 | tf_op jit(solution)/shard_map/ppermute | solution.py:263
  204.4 68.2 %all-to-all-start.2 = ((bf16[16,1024,128]{2,1,0:T(8,128)(2,1)}), bf16[16,1024,128]{2,1,0:T(8,128)(2,1)}, u32[]{:S(2)}, u32[]{:S(2)}) async-start(bf16[16,1024,128]{2,1,0:T(8,128)(2,1)} %shard_map.80), calls=%async_computation.2 | async-start | bytes 8388608 | tf_op jit(solution)/shard_map/all_to_all | solution.py:315

commit v5 on v3

--- a/solution.py
+++ b/solution.py
@@ -167,34 +167,47 @@
     )(ga, xa, gb, xb)
 
 
-def row_body(wt_ref, g_ref, out_ref):
+def row_body(first, wt_ref, g_ref, pack_ref, *refs):
+    if first:
+        (out_ref,) = refs
+    else:
+        back_ref, out_ref = refs
     for q in range(D // 256):
-        back = jnp.dot(
-            wt_ref[q * 256 : (q + 1) * 256, :], g_ref[...], preferred_element_type=F32
-        ).astype(BF16)
+        rows = slice(q * 256, (q + 1) * 256)
+        mine = jnp.dot(wt_ref[rows, :], g_ref[...], preferred_element_type=F32)
         for d in range(STEP):
-            out_ref[d, q * 256 : (q + 1) * 256, :] = back[:, d * ROWS : (d + 1) * ROWS]
-
-
-def row_grad(wt, g):
+            part = mine[:, d * ROWS : (d + 1) * ROWS]
+            if not first:
+                part = part + back_ref[d, rows, :].astype(F32)
+            out_ref[d, rows, :] = part.astype(BF16)
+    out_ref[:, D : D + BS, :] = pack_ref[...]
+    if not first:
+        out_ref[:, D + BS :, :] = back_ref[:, D:, :]
+
+
+def row_grad(wt, g, pack, back=None):
+    first = back is None
     count = g.shape[1] // ROWS
+    height = D + BS if first else D + 2 * BS
     return pl.pallas_call(
-        row_body,
+        functools.partial(row_body, first),
         grid=(count // STEP,),
         in_specs=[
             pl.BlockSpec((D, COLS), lambda i: (0, 0)),
             pl.BlockSpec((COLS, STEP * ROWS), lambda i: (0, i)),
-        ],
-        out_specs=pl.BlockSpec((STEP, D, ROWS), lambda i: (i, 0, 0)),
-        out_shape=jax.ShapeDtypeStruct((count, D, ROWS), BF16),
+            pl.BlockSpec((STEP, BS, ROWS), lambda i: (i, 0, 0)),
+        ]
+        + ([] if first else [pl.BlockSpec((STEP, D + BS, ROWS), lambda i: (i, 0, 0))]),
+        out_specs=pl.BlockSpec((STEP, height, ROWS), lambda i: (i, 0, 0)),
+        out_shape=jax.ShapeDtypeStruct((count, height, ROWS), BF16),
         compiler_params=pltpu.CompilerParams(vmem_limit_bytes=VMEM),
         cost_estimate=pl.CostEstimate(
-            flops=2 * count * ROWS * COLS * D, bytes_accessed=9 * 2**20, transcendentals=0
-        ),
-    )(wt, g)
-
-
-def unpack_body(key_ref, got_ref, out_ref):
+            flops=2 * count * ROWS * COLS * D, bytes_accessed=12 * 2**20, transcendentals=0
+        ),
+    )(wt, g, pack, *([] if first else [back]))
+
+
+def finish_body(key_ref, rows_ref, pack_ref, gx_ref, out_ref):
     key = key_ref[...]
     lane = lax.broadcasted_iota(jnp.int32, (1, 2 * ROWS), 1)
     total = jnp.zeros(out_ref.shape, F32)
@@ -206,7 +219,7 @@
                 [
                     jnp.concatenate(
                         [
-                            got_ref[2 * owner + h, base + hh * HALF : base + (hh + 1) * HALF, :]
+                            pack_ref[2 * owner + h, base + hh * HALF : base + (hh + 1) * HALF, :]
                             for hh in range(2)
                         ],
                         axis=1,
@@ -218,25 +231,37 @@
             pick = jnp.where(key == lane + chunk * 2 * ROWS, 1.0, 0.0).astype(BF16)
             total += lax.dot_general(pick, table, NT, preferred_element_type=F32)
     out_ref[...] = total.astype(BF16)
-
-
-def unpack(key, got):
-    pairs = key.shape[0]
-    block = 512
+    for q in range(3):
+        rows = slice(q * ROWS, (q + 1) * ROWS)
+        part = rows_ref[0, rows, :].astype(F32)
+        for i in range(1, 16):
+            part = part + rows_ref[i, rows, :].astype(F32)
+        gx_ref[:, rows] = part.T.astype(BF16)
+
+
+def finish(key, got):
+    pairs, block, deep = key.shape[0], 1024, D // 2
     return pl.pallas_call(
-        unpack_body,
-        grid=(pairs // block,),
+        finish_body,
+        grid=(2,),
         in_specs=[
             pl.BlockSpec((block, 2 * ROWS), lambda i: (i, 0)),
-            pl.BlockSpec(got.shape, lambda i: (0, 0, 0)),
-        ],
-        out_specs=pl.BlockSpec((block, BS), lambda i: (i, 0)),
-        out_shape=jax.ShapeDtypeStruct((pairs, BS), BF16),
+            pl.BlockSpec((16, deep, ROWS), lambda i: (0, i, 0)),
+            pl.BlockSpec((16, 2 * BS, ROWS), lambda i: (0, 3, 0)),
+        ],
+        out_specs=[
+            pl.BlockSpec((ROWS, deep), lambda i: (0, i)),
+            pl.BlockSpec((block, BS), lambda i: (i, 0)),
+        ],
+        out_shape=[
+            jax.ShapeDtypeStruct((ROWS, D), BF16),
+            jax.ShapeDtypeStruct((pairs, BS), BF16),
+        ],
         compiler_params=pltpu.CompilerParams(vmem_limit_bytes=VMEM),
         cost_estimate=pl.CostEstimate(
             flops=2 * pairs * 4096 * BS, bytes_accessed=8 * 2**20, transcendentals=0
         ),
-    )(key, got)
+    )(key, got, got)
 
 
 def shards(features, weights, block_ids, label_codes, counts):
@@ -244,6 +269,7 @@
     core = lax.axis_index("core")
     meta = jnp.stack([8 * core + inst // 2, inst % 2]).astype(jnp.int32)
     mine = lax.dynamic_slice_in_dim(weights, inst * HALF, HALF, 0)
+    mine, features, block_ids = lax.optimization_barrier((mine, features, block_ids))
     w = lax.all_gather(mine, "z").reshape(COLS, D)
 
     alive = jnp.arange(TOP, dtype=jnp.int32)[None, :] < counts[:, None]
@@ -251,28 +277,25 @@
     slots = jnp.concatenate([block_ids.T, code.T], axis=1).astype(BF16)
     slots = jnp.pad(slots, ((0, 0), (0, D - 2 * ROWS)))
     sent = jnp.concatenate([features, slots], axis=0)
-    copies = jnp.broadcast_to(sent[None], (Z,) + sent.shape)
+    copies = jnp.broadcast_to(sent[None], (16,) + sent.shape)
     own = lax.all_to_all(copies, PLANE, split_axis=0, concat_axis=0, tiled=True)
     swap = [(0, 1), (1, 0)]
     own, w = lax.optimization_barrier((own, w))
     wt = w.T
     other = lax.ppermute(own, "core", swap)
     own_grad, own_pack = expert(meta, own, w)
+    other, own_grad = lax.optimization_barrier((other, own_grad))
     other_grad, other_pack = expert(meta, other, w)
-    other_rows = row_grad(wt, other_grad)
-    other_rows, own_grad = lax.optimization_barrier((other_rows, own_grad))
-    back_rows = lax.ppermute(other_rows, "core", swap)
-    back_pack = lax.ppermute(other_pack, "core", swap)
+    other_out = row_grad(wt, other_grad, other_pack)
+    back = lax.ppermute(other_out, "core", swap)
+    other_out, own_grad = lax.optimization_barrier((other_out, own_grad))
     total = weight_grad(own_grad, own, other_grad, other)
     total, own_grad = lax.optimization_barrier((total, own_grad))
     grad_w = lax.psum_scatter(
         total.reshape(Z, HALF, D), "z", scatter_dimension=0, tiled=False
-    ).astype(F32)
-    packs = jnp.concatenate([own_pack, back_pack], axis=1)
-    got = lax.all_to_all(packs, PLANE, split_axis=0, concat_axis=0, tiled=True)
-    sums = (row_grad(wt, own_grad).astype(F32) + back_rows.astype(F32)).astype(BF16)
-    got_rows = lax.all_to_all(sums, PLANE, split_axis=0, concat_axis=0, tiled=True)
-    grad_x = jnp.sum(got_rows, axis=0, dtype=F32).T.astype(BF16)
+    )
+    payload = row_grad(wt, own_grad, own_pack, back)
+    got = lax.all_to_all(payload, PLANE, split_axis=0, concat_axis=0, tiled=True)
 
     blocks = jnp.arange(256, dtype=jnp.int32)
     named = (block_ids[:, :, None] == blocks).any(axis=1).astype(BF16)
@@ -286,7 +309,10 @@
     crossed = (owner // 8) ^ core
     key = (((owner % 8) * 2 + crossed) * 2 + row // 8) * ROWS + (row % 8) * MOST + rank
     key = jnp.broadcast_to(key.reshape(-1, 1), (ROWS * TOP, 2 * ROWS))
-    grad_logits = unpack(key, got).reshape(ROWS, TOP, BS)
+    grad_x, grad_logits = finish(key, got)
+    grad_logits = grad_logits.reshape(ROWS, TOP, BS)
+    grad_w, grad_x = lax.optimization_barrier((grad_w, grad_x))
+    grad_w = grad_w.astype(F32)
     return (grad_x, grad_w, grad_logits)
 
 

time: 239 us -> 239 us (level)
  waiting for transfers between devices: 123 us -> 139 us
  starting transfers between devices: 31.2 us -> 22.1 us
  other arithmetic: 13.6 us -> 5.57 us
    all_to_all x2 -> x1, waiting for transfers between devices: 0.01 us -> 56.8 us  [shards(): lax.all_to_all(payload, PLANE, split_axis=0, concat_axis=0, tiled=True)]
    reduce_scatter x1, waiting for transfers between devices: 42.3 us -> 4.9 us  [shards(): lax.psum_scatter(total.reshape(Z, HALF, D), 'z', scatter_dimension=0, til...]
    all_to_all x2 -> x1, starting transfers between devices: 14.6 us -> 7.37 us  [shards(): lax.all_to_all(payload, PLANE, split_axis=0, concat_axis=0, tiled=True)]
    convert_element_type x2 -> x1, other arithmetic: 5.92 us -> 1.58 us  [shards(): grad_w = grad_w.astype(F32)]
    ppermute x2 -> x1, waiting for transfers between devices: 4.09 us -> 0.01 us  [shards(): back = lax.ppermute(other_out, 'core', swap)]
  transfers between devices with their start and end apart: 8 -> 6, of which waited for: 3 -> 3; matrix products, arithmetic and copies ran while one was open for 5% -> 2% of each run, Pallas kernels for 14% -> 12%
where the time goes in v5:
time: 239 us; the launch traced here: 238 us
  waiting for transfers between devices  139 us (58%)
  Pallas kernels  49.2 us (21%)
  starting transfers between devices  22.1 us (9%)
  between operations  14.2 us (6%)
  local copies, waits for them, and re-layouts  7.26 us (3%)
  other arithmetic  5.57 us (2%)
    all_gather x1, waiting for transfers between devices, shards(): w = lax.all_gather(mine, 'z').reshape(COLS, D)  76.4 us
    all_to_all x1, waiting for transfers between devices, shards(): lax.all_to_all(payload, PLANE, split_axis=0, concat_axis=0, tiled=True)  56.8 us
    pallas_call x2, Pallas kernels, expert(): pl.pallas_call(expert_body, grid_spec=pltpu.PrefetchScalarGridSpec(num_sc...  17.1 us
    pallas_call x1, Pallas kernels, weight_grad(): pl.pallas_call(weight_body, grid=(2 * half,), in_specs=[pl.BlockSpec((COL...  12.4 us
    pallas_call x2, Pallas kernels, row_grad(): pl.pallas_call(functools.partial(row_body, first), grid=(count // STEP,),...  12.4 us
    all_to_all x1, starting transfers between devices, shards(): own = lax.all_to_all(copies, PLANE, split_axis=0, concat_axis=0, tiled=True)  10.2 us
    pallas_call x1, Pallas kernels, finish(): pl.pallas_call(finish_body, grid=(2,), in_specs=[pl.BlockSpec((block, 2 *...  7.39 us
    all_to_all x1, starting transfers between devices, shards(): lax.all_to_all(payload, PLANE, split_axis=0, concat_axis=0, tiled=True)  7.37 us
  transfers between devices with their start and end apart: 6, of which 3 were waited for; matrix products, arithmetic and copies ran while one was open for 2% of the time, Pallas kernels for 12%

profile of v5, /device:TPU:2, one launch (start us, length us, event | category | flops | bytes accessed | tf_op | source)
XLA Modules:
  0.0 237.8 jit_solution(10980501649770781478)
XLA Ops:
  7.2 0.0 copy-start
  7.2 0.9 copy.29
  8.1 0.7 fusion.23
  8.8 0.1 copy.30
  8.9 0.0 copy-done
  8.9 0.7 constant_dynamic-slice_fusion
  9.6 0.7 convert_bitcast_fusion
  10.3 0.9 pad_maximum_fusion
  11.2 2.0 broadcast_in_dim.23
  13.2 10.2 %all-to-all-start = ((bf16[16,144,768]{2,1,0:T(8,128)(2,1)}), bf16[16,144,768]{2,1,0:T(8,128)(2,1)}, u32[]{:S(2)}, u32[]{:S(2)}) async-start(bf16[16,144,768]{2,1,0:T(8,128)(2,1)} %broadcast_in_dim.23), calls=%async_computation | async-start | bytes 7077888 | tf_op jit(solution)/shard_map/all_to_all | solution.py:281
  23.4 0.0 all-gather.3.cloned.1.call-start
  23.4 0.7 all-gather.3.cloned.1.call-update
  24.1 76.4 %all-gather.3.cloned.1.call-done.w_ref = bf16[1024,768]{1,0:T(8,128)(2,1)} async-done(((bf16[64,768]{1,0:T(8,128)(2,1)}), bf16[1024,768]{1,0:T(8,128)(2,1)}) %all-gather.3.cloned.1.call-update) | async-done | bytes 1572880 | tf_op jit(solution)/shard_map/all_gather | solution.py:273
  100.5 0.0 all-to-all-done.x_ref.xa_ref
  100.5 1.9 collective-permute-start
  102.4 0.1 pad_add_fusion.meta
  102.5 1.7 copy.31
  104.2 0.0 copy-start.1
  104.2 1.4 copy-done.1
  105.6 8.6 %shard_map.76 = (bf16[1024,2048]{1,0:T(8,128)(2,1)}, bf16[16,128,128]{2,1,0:T(8,128)(2,1)S(1)}) custom-call(s32[2]{0:T(128)S(1)} %pad_add_fusion.meta, bf16[16,144,768]{2,1,0:T(8,128)(2,1)} %all-to-all-done.x_ref.xa_ref, bf16[1024,768]{1,0:T(8,128)(2,1)S(1)} %copy-done.1), custom_call_target="tpu_custom_call" | custom-call | flops 3221225472 | bytes 10485760 | tf_op jit(solution)/shard_map/pallas_call | solution.py:93
  114.2 0.0 collective-permute-done.x_ref.xb_ref
  114.2 8.5 %shard_map.77 = (bf16[1024,2048]{1,0:T(8,128)(2,1)}, bf16[16,128,128]{2,1,0:T(8,128)(2,1)S(1)}) custom-call(s32[2]{0:T(128)S(1)} %pad_add_fusion.meta, bf16[16,144,768]{2,1,0:T(8,128)(2,1)} %collective-permute-done.x_ref.xb_ref, bf16[1024,768]{1,0:T(8,128)(2,1)S(1)} %copy-done.1), custom_call_target="tpu_custom_call" | custom-call | flops 3221225472 | bytes 10485760 | tf_op jit(solution)/shard_map/pallas_call | solution.py:93
  122.7 5.5 %shard_map.78 = bf16[16,896,128]{2,1,0:T(8,128)(2,1)S(1)} custom-call(bf16[768,1024]{1,0:T(8,128)(2,1)S(1)} %bitcast.11, bf16[1024,2048]{1,0:T(8,128)(2,1)} %get-tuple-element.28.g_ref.gb_ref, bf16[16,128,128]{2,1,0:T(8,128)(2,1)S(1)} %get-tuple-element.29.pack_ref), custom_call_target="tpu_custom_call" | custom-call | flops 3221225472 | bytes 12582912 | tf_op jit(solution)/shard_map/pallas_call | solution.py:192
  128.2 2.4 %collective-permute-start.1 = (bf16[16,896,128]{2,1,0:T(8,128)(2,1)S(1)}, bf16[16,896,128]{2,1,0:T(8,128)(2,1)S(1)}, u32[]{:S(2)}, u32[]{:S(2)}) collective-permute-start(bf16[16,896,128]{2,1,0:T(8,128)(2,1)S(1)} %shard_map.78), channel_id=1, source_target_pairs={{0,1},{1,0},{2,3},{3,2},{4,5},{5,4},{6,7},{7,6},{8,9},{9,8},{10,11... | collective-permute-start | bytes 11010056 | tf_op jit(solution)/shard_map/ppermute | solution.py:290
  130.6 12.4 %shard_map.79 = bf16[1024,768]{1,0:T(8,128)(2,1)} custom-call(bf16[1024,2048]{1,0:T(8,128)(2,1)} %get-tuple-element.33.ga_ref.g_ref, bf16[16,144,768]{2,1,0:T(8,128)(2,1)} %all-to-all-done.x_ref.xa_ref, bf16[1024,2048]{1,0:T(8,128)(2,1)} %get-tuple-element.28.g_ref.gb_ref, bf16[16,144,768]{2,1,0:T(8,128)(2,1)} %collective-permute-done.x_ref.xb_ref), custom_call_target="tpu_custom_call" | custom-call | flops 6442450944 | bytes 18874368 | tf_op jit(solution)/shard_map/pallas_call | solution.py:151
  143.0 0.0 collective-permute-done.1.refs_0_
  143.0 6.9 %shard_map.80 = bf16[16,1024,128]{2,1,0:T(8,128)(2,1)} custom-call(bf16[768,1024]{1,0:T(8,128)(2,1)S(1)} %bitcast.12, bf16[1024,2048]{1,0:T(8,128)(2,1)} %get-tuple-element.33.ga_ref.g_ref, bf16[16,128,128]{2,1,0:T(8,128)(2,1)S(1)} %get-tuple-element.34.pack_ref, bf16[16,896,128]{2,1,0:T(8,128)(2,1)S(1)} %collective-permute-done.1.refs_0_), custom_call_target="tpu_custom_call" | custom-call | flops 3221225472 | bytes 12582912 | tf_op jit(solution)/shard_map/pallas_call | solution.py:192
  149.9 0.0 copy-start.2
  149.9 7.4 %all-to-all-start.1 = ((bf16[16,1024,128]{2,1,0:T(8,128)(2,1)}), bf16[16,1024,128]{2,1,0:T(8,128)(2,1)}, u32[]{:S(2)}, u32[]{:S(2)}) async-start(bf16[16,1024,128]{2,1,0:T(8,128)(2,1)} %shard_map.80), calls=%async_computation.2 | async-start | bytes 8388608 | tf_op jit(solution)/shard_map/all_to_all | solution.py:298
  157.3 0.2 reduce-scatter.2.cloned.1.call-start
  157.5 0.5 reduce-scatter.2.cloned.1.call-update
  158.0 0.0 copy-done.2
  158.0 0.1 copy.32
  158.1 0.6 fusion
  158.7 0.2 fusion.19
  158.9 0.7 select_reduce_fusion
  159.6 0.2 fusion.7
  159.8 0.1 broadcast_in_dim.42
  159.9 56.8 %all-to-all-done.1.rows_ref.pack_ref = bf16[16,1024,128]{2,1,0:T(8,128)(2,1)} async-done(((bf16[16,1024,128]{2,1,0:T(8,128)(2,1)}), bf16[16,1024,128]{2,1,0:T(8,128)(2,1)}, u32[]{:S(2)}, u32[]{:S(2)}) %all-to-all-start.1) | async-done | bytes 4194336 | tf_op jit(solution)/shard_map/all_to_all | solution.py:298
  216.8 0.3 broadcast_in_dim.43.key_ref
  217.1 7.4 %shard_map.81 = (bf16[128,768]{1,0:T(8,128)(2,1)}, bf16[2048,128]{1,0:T(8,128)(2,1)}) custom-call(s32[2048,256]{1,0:T(8,128)S(1)} %broadcast_in_dim.43.key_ref, bf16[16,1024,128]{2,1,0:T(8,128)(2,1)} %all-to-all-done.1.rows_ref.pack_ref, bf16[16,1024,128]{2,1,0:T(8,128)(2,1)} %all-to-all-done.1.rows_ref.pack_ref), custom_call_target="tpu_custom_call" | custom-call | flops 2147483648 | bytes 8388608 | tf_op jit(solution)/shard_map/pallas_call | solution.py:244
  224.5 4.9 %reduce-scatter.2.cloned.1.call-done = bf16[1,64,768]{2,1,0:T(8,128)(2,1)} async-done(((bf16[16,64,768]{2,1,0:T(8,128)(2,1)}), bf16[1,64,768]{2,1,0:T(8,128)(2,1)}) %reduce-scatter.2.cloned.1.call-update) | async-done | bytes 98320 | tf_op jit(solution)/shard_map/reduce_scatter | solution.py:294
  229.4 1.6 convert_element_type.12
  (1 shorter events, 0.0 us)
Async XLA Ops:
  7.2 1.7 copy-start
  13.2 87.3 %all-to-all-start = ((bf16[16,144,768]{2,1,0:T(8,128)(2,1)}), bf16[16,144,768]{2,1,0:T(8,128)(2,1)}, u32[]{:S(2)}, u32[]{:S(2)}) async-start(bf16[16,144,768]{2,1,0:T(8,128)(2,1)} %broadcast_in_dim.23), calls=%async_computation | async-start | bytes 7077888 | tf_op jit(solution)/shard_map/all_to_all | solution.py:281
  23.4 77.1 %all-gather.3.cloned.1.call-start = ((), (), s32[]{:S(2)}) async-start(), calls=%async_computation.4 | async-start | bytes 1671168 | tf_op jit(solution)/shard_map/all_gather | solution.py:273
  100.5 13.7 %collective-permute-start = (bf16[16,144,768]{2,1,0:T(8,128)(2,1)}, bf16[16,144,768]{2,1,0:T(8,128)(2,1)}, u32[]{:S(2)}, u32[]{:S(2)}) collective-permute-start(bf16[16,144,768]{2,1,0:T(8,128)(2,1)} %all-to-all-done.x_ref.xa_ref), channel_id=1, source_target_pairs={{0,1},{1,0},{2,3},{3,2},{4,5},{5,4},{6,7},{7,6},{8,9},{9,8},{10,11... | collective-permute-start | bytes 10616840 | tf_op jit(solution)/shard_map/ppermute | solution.py:285
  104.2 1.4 copy-start.1
  128.2 14.8 %collective-permute-start.1 = (bf16[16,896,128]{2,1,0:T(8,128)(2,1)S(1)}, bf16[16,896,128]{2,1,0:T(8,128)(2,1)S(1)}, u32[]{:S(2)}, u32[]{:S(2)}) collective-permute-start(bf16[16,896,128]{2,1,0:T(8,128)(2,1)S(1)} %shard_map.78), channel_id=1, source_target_pairs={{0,1},{1,0},{2,3},{3,2},{4,5},{5,4},{6,7},{7,6},{8,9},{9,8},{10,11... | collective-permute-start | bytes 11010056 | tf_op jit(solution)/shard_map/ppermute | solution.py:290
  149.9 8.1 %copy-start.2 = (s32[128,16]{0,1:T(8,128)S(1)}, s32[128,16]{0,1:T(8,128)}, u32[]{:S(2)}) copy-start(s32[128,16]{0,1:T(8,128)} %param.7) | copy-start | bytes 24580
  149.9 66.9 %all-to-all-start.1 = ((bf16[16,1024,128]{2,1,0:T(8,128)(2,1)}), bf16[16,1024,128]{2,1,0:T(8,128)(2,1)}, u32[]{:S(2)}, u32[]{:S(2)}) async-start(bf16[16,1024,128]{2,1,0:T(8,128)(2,1)} %shard_map.80), calls=%async_computation.2 | async-start | bytes 8388608 | tf_op jit(solution)/shard_map/all_to_all | solution.py:298
  157.3 72.1 %reduce-scatter.2.cloned.1.call-start = ((), (), s32[]{:S(2)}) async-start(), calls=%async_computation.3 | async-start | bytes 1671168 | tf_op jit(solution)/shard_map/reduce_scatter | solution.py:294
Sparse Core Ops, SparseCore 0:
  26.9 73.5 all-gather.2
  160.9 68.4 reduce-scatter.1
